TPU v7x, 128 devices: a whole 4x4x4 slice. The times are simulated.
128 devices in a mesh: seq: 32 (over z, y_hi, x), chan: 4 (over y_lo, core).
Axes of the slice: x: 4, y: 4 (y_hi: 2, y_lo: 2; y = y_hi * 2 + y_lo), z: 4, core: 2. Of those that a mesh axis runs over, the one named last changes fastest.
Arguments:
- tokens: bfloat16 [131072, 4096], P('seq', 'chan'), may hold values from -170 to 170
- norm_gain: bfloat16 [4096], P('chan'), may hold values from 0.099609375 to 1.8984375
- first_factor: bfloat16 [512, 512], replicated, may hold values from -0.25 to 0.25
- twiddle_in: bfloat16 [256, 512], P('seq'), may hold values from -4 to 4
- second_factor: bfloat16 [256, 256], replicated, may hold values from -0.375 to 0.375
- kernel_gate: bfloat16 [256, 512, 4096], P(None, 'seq', 'chan'), may hold values from -4 to 4
- second_inverse: bfloat16 [256, 256], replicated, may hold values from -0.375 to 0.375
- twiddle_out: bfloat16 [256, 512], P(None, 'seq'), may hold values from -4 to 4
- first_inverse: bfloat16 [512, 512], replicated, may hold values from -0.25 to 0.25
Outputs:
- mixed: bfloat16 [131072, 4096], P('seq', 'chan')
All inputs are finite; a program needn't handle non-finite values.
Results may differ from a plain program's by a relative error of at most 0.007.
Values may be sent and summed in bfloat16 or wider, within the bound.
No kernel may reach another device: no remote copies, remote signals or barrier semaphores. Data moves between devices by JAX's collectives and lax.ppermute only.
A program may use at most 192 MiB of HBM per device.

v0:
```python
import jax
import jax.numpy as jnp
from jax import lax
from jax.sharding import PartitionSpec as P


def first_section(values, first_factor, twiddle):
    result = jnp.einsum("kq,pqc->pkc", first_factor, values, preferred_element_type=jnp.float32)
    return (result * twiddle.astype(jnp.float32)[:, :, None]).astype(jnp.bfloat16)


def middle(values, second_factor, gate_block, second_inverse, twiddle):
    gated = jnp.einsum("mp,pkc->mkc", second_factor, values, preferred_element_type=jnp.float32)
    gated = (gated * gate_block.astype(jnp.float32)).astype(jnp.bfloat16)
    back = jnp.einsum("nm,mkc->nkc", second_inverse, gated, preferred_element_type=jnp.float32)
    return (back * twiddle.astype(jnp.float32)[:, :, None]).astype(jnp.bfloat16)


def last_section(values, first_inverse):
    result = jnp.einsum("qk,nkc->nqc", first_inverse, values, preferred_element_type=jnp.float32)
    return result.astype(jnp.bfloat16)


def per_device(
    tokens,
    norm_gain,
    first_factor,
    twiddle_in,
    second_factor,
    kernel_gate,
    second_inverse,
    twiddle_out,
    first_inverse,
):
    seq_count = lax.axis_size("seq")
    rows_dev, width_dev = tokens.shape
    q_order = first_factor.shape[0]
    p_order = second_factor.shape[0]
    p_block = p_order // seq_count
    widened = tokens.astype(jnp.float32)
    square = lax.psum(jnp.sum(widened * widened, axis=1), "chan")
    inverse_rms = lax.rsqrt(square / (width_dev * lax.axis_size("chan")) + 1e-05)
    normed = (widened * inverse_rms[:, None] * norm_gain.astype(jnp.float32)).astype(jnp.bfloat16)
    normed = normed.reshape(p_block, q_order, width_dev)
    first = first_section(normed, first_factor, twiddle_in)
    columns = lax.all_to_all(first, "seq", split_axis=1, concat_axis=0, tiled=True)
    inverse_part = middle(columns, second_factor, kernel_gate, second_inverse, twiddle_out)
    returned = lax.all_to_all(inverse_part, "seq", split_axis=0, concat_axis=1, tiled=True)
    mixed_out = last_section(returned, first_inverse)
    return mixed_out.reshape(rows_dev, width_dev)


def solution(mesh):
    return jax.shard_map(
        per_device,
        mesh=mesh,
        in_specs=(
            P("seq", "chan"),
            P("chan"),
            P(),
            P("seq", None),
            P(),
            P(None, "seq", "chan"),
            P(),
            P(None, "seq"),
            P(),
        ),
        out_specs=P("seq", "chan"),
        check_vma=False,
    )
```

profile of v0, /device:TPU:1, one launch (start us, length us, event | category | flops | bytes accessed | tf_op | source)
XLA Modules:
  0.0 343.7 jit_solution(17054480421215849497)
XLA Ops:
  0.0 0.0 copy-start
  0.0 0.7 convert_element_type.37
  0.7 0.7 convert_element_type.39
  1.4 5.1 %fusion = f32[4096]{0:T(1024)S(1)} fusion(bf16[4096,1024]{1,0:T(8,128)(2,1)} %param.9), kind=kLoop, calls=%fused_computation.2 | loop fusion | flops 12578816 | bytes 8404992 | tf_op jit(solution)/shard_map/reduce_sum | solution.py:41
  6.5 10.5 %psum.7 = f32[4096]{0:T(1024)S(1)} all-reduce(f32[4096]{0:T(1024)S(1)} %fusion), channel_id=1, replica_groups=mesh['seq'=32,'chan'=4] {'chan'}, use_global_device_ids=true, to_apply=%region_1.0 | all-reduce | flops 4096 | bytes 32768 | tf_op jit(solution)/shard_map/psum | solution.py:41
  17.1 5.1 %fusion.2 = bf16[4096,1024]{1,0:T(8,128)(2,1)S(1)} fusion(bf16[4096,1024]{1,0:T(8,128)(2,1)} %param.9, f32[1024]{0:T(1024)S(1)} %convert_element_type.37, f32[4096]{0:T(1024)S(1)} %add_rsqrt_fusion), kind=kLoop, calls=%fused_computation.4 | loop fusion | flops 16777216 | bytes 16797696 | tf_op jit(solution)/shard_map/convert_element_type | solution.py:43
  22.2 0.0 copy-done
  22.2 7.0 %fusion.6 = bf16[8,512,1024]{1,2,0:T(8,128)(2,1)} fusion(f32[8,512]{1,0:T(8,128)S(1)} %convert_element_type.39, bf16[8,512,1024]{2,1,0:T(8,128)(2,1)S(1)} %bitcast.40, bf16[512,512]{1,0:T(8,128)(2,1)S(1)} %copy-done), kind=kOutput, calls=%fused_computation.12 | convolution fusion | flops 4303355904 | bytes 17317888 | tf_op jit(solution)/shard_map/kq,pqc->pkc/dot_general | solution.py:8
  29.1 12.6 %copy.20 = bf16[8,512,1024]{2,0,1:T(8,128)(2,1)} copy(bf16[8,512,1024]{1,2,0:T(8,128)(2,1)} %fusion.6) | data formatting | bytes 16777216 | tf_op jit(solution)/shard_map/convert_element_type | solution.py:9
  41.8 0.0 copy-start.2
  41.8 11.0 %all-to-all-start = ((bf16[8,512,1024]{2,0,1:T(8,128)(2,1)}), bf16[8,512,1024]{2,0,1:T(8,128)(2,1)}, u32[]{:S(2)}, u32[]{:S(2)}) async-start(bf16[8,512,1024]{2,0,1:T(8,128)(2,1)} %copy.20), calls=%async_computation | async-start | bytes 16777216 | tf_op jit(solution)/shard_map/all_to_all | solution.py:46
  52.8 0.0 copy-done.2
  52.8 12.3 %copy.24 = bf16[256,16,1024]{0,2,1:T(8,128)(2,1)} copy(bf16[256,16,1024]{2,1,0:T(8,128)(2,1)} %param.14) | data formatting | bytes 16777216 | tf_op args[5]
  65.0 95.9 %all-to-all-done = bf16[8,512,1024]{2,0,1:T(8,128)(2,1)} async-done(((bf16[8,512,1024]{2,0,1:T(8,128)(2,1)}), bf16[8,512,1024]{2,0,1:T(8,128)(2,1)}, u32[]{:S(2)}, u32[]{:S(2)}) %all-to-all-start) | async-done | bytes 8388640 | tf_op jit(solution)/shard_map/all_to_all | solution.py:46
  160.9 15.2 %copy.22 = bf16[32,8,16,1024]{3,2,1,0:T(8,128)(2,1)} copy(bf16[32,8,16,1024]{3,1,2,0:T(8,128)(2,1)} %bitcast.5) | data formatting | bytes 16777216 | tf_op jit(solution)/shard_map/all_to_all | solution.py:46
  176.1 0.0 copy-done.4
  176.2 0.0 copy-done.5
  176.2 24.0 %fusion.3 = bf16[256,16,1024]{0,2,1:T(8,128)(2,1)} fusion(f32[256,16]{0,1:T(8,128)S(1)} %convert_element_type.44, bf16[256,16,1024]{0,2,1:T(8,128)(2,1)} %copy.24, bf16[256,16,1024]{2,1,0:T(8,128)(2,1)} %bitcast.41, bf16[256,256]{1,0:T(8,128)(2,1)S(1)} %copy-done.4, bf16[256,256]{1,0:T(8,128)(2,1)S(1)} %copy-done.5), kind=kOutput, calls=%fused_computation.6 | convolution fusion | flops 4315938816 | bytes 25444352 | tf_op jit(solution)/shard_map/nm,mkc->nkc/dot_general | solution.py:15
  200.2 12.2 %copy.25 = bf16[256,16,1024]{2,1,0:T(8,128)(2,1)} copy(bf16[256,16,1024]{0,2,1:T(8,128)(2,1)} %fusion.3) | data formatting | bytes 16777216 | tf_op jit(solution)/shard_map/convert_element_type | solution.py:16
  212.4 112.5 %all_to_all.36 = bf16[256,16,1024]{2,1,0:T(8,128)(2,1)} all-to-all(bf16[256,16,1024]{2,1,0:T(8,128)(2,1)} %copy.25), channel_id=1, replica_groups=mesh['seq'=32,'chan'=4] {'seq'}, dimensions={0} | all-to-all | bytes 16777216 | tf_op jit(solution)/shard_map/all_to_all | solution.py:48
  324.9 8.6 %copy.26 = bf16[8,32,16,1024]{3,2,1,0:T(8,128)(2,1)} copy(bf16[8,32,16,1024]{3,2,0,1:T(8,128)(2,1)} %bitcast.39) | data formatting | bytes 16777216 | tf_op jit(solution)/shard_map/all_to_all | solution.py:48
  333.5 0.0 copy-done.3
  333.5 10.2 %convolution_convert_fusion = bf16[8,1024,512]{1,2,0:T(8,128)(2,1)} fusion(bf16[8,512,1024]{2,1,0:T(8,128)(2,1)} %bitcast.42, bf16[512,512]{1,0:T(8,128)(2,1)S(1)} %copy-done.3), kind=kOutput, calls=%fused_computation.11 | convolution fusion | flops 4299161600 | bytes 17301504 | tf_op jit(solution)/shard_map/qk,nkc->nqc/dot_general | solution.py:20
  343.7 0.0 copy-done.1
  (6 shorter events, 0.0 us)
Async XLA Ops:
  0.0 22.2 %copy-start = (bf16[512,512]{1,0:T(8,128)(2,1)S(1)}, bf16[512,512]{1,0:T(8,128)(2,1)}, u32[]{:S(2)}) copy-start(bf16[512,512]{1,0:T(8,128)(2,1)} %param.11) | copy-start | bytes 1572868
  41.8 11.0 %copy-start.2 = (bf16[256,16]{0,1:T(8,128)(2,1)S(1)}, bf16[256,16]{0,1:T(8,128)(2,1)}, u32[]{:S(2)}) copy-start(bf16[256,16]{0,1:T(8,128)(2,1)} %param.16) | copy-start | bytes 24580
  41.8 119.2 %all-to-all-start = ((bf16[8,512,1024]{2,0,1:T(8,128)(2,1)}), bf16[8,512,1024]{2,0,1:T(8,128)(2,1)}, u32[]{:S(2)}, u32[]{:S(2)}) async-start(bf16[8,512,1024]{2,0,1:T(8,128)(2,1)} %copy.20), calls=%async_computation | async-start | bytes 16777216 | tf_op jit(solution)/shard_map/all_to_all | solution.py:46
  160.9 15.2 %copy-start.4 = (bf16[256,256]{1,0:T(8,128)(2,1)S(1)}, bf16[256,256]{1,0:T(8,128)(2,1)}, u32[]{:S(2)}) copy-start(bf16[256,256]{1,0:T(8,128)(2,1)} %param.15) | copy-start | bytes 393220
  160.9 15.2 %copy-start.5 = (bf16[256,256]{1,0:T(8,128)(2,1)S(1)}, bf16[256,256]{1,0:T(8,128)(2,1)}, u32[]{:S(2)}) copy-start(bf16[256,256]{1,0:T(8,128)(2,1)} %param.13) | copy-start | bytes 393220
  324.9 8.6 %copy-start.3 = (bf16[512,512]{1,0:T(8,128)(2,1)S(1)}, bf16[512,512]{1,0:T(8,128)(2,1)}, u32[]{:S(2)}) copy-start(bf16[512,512]{1,0:T(8,128)(2,1)} %param.17) | copy-start | bytes 1572868
  333.5 10.2 %copy-start.1 = (bf16[512,512]{1,0:T(8,128)(2,1)S(1)}, bf16[512,512]{1,0:T(8,128)(2,1)}, u32[]{:S(2)}) copy-start(bf16[512,512]{1,0:T(8,128)(2,1)} %param.11) | copy-start | bytes 1572868
where the time goes:
time: 348 us; the launch traced here: 344 us
  blocking collectives  123 us (35%)
  waiting for transfers between devices  95.9 us (28%)
  local copies, waits for them, and re-layouts  60.9 us (18%)
  matrix products  41.1 us (12%)
  other arithmetic  11.6 us (3%)
  starting transfers between devices  11 us (3%)
    all_to_all x1, blocking collectives, per_device(): lax.all_to_all(inverse_part, 'seq', split_axis=0, concat_axis=1, tiled=True)  113 us
    all_to_all x1, waiting for transfers between devices, per_device(): lax.all_to_all(first, 'seq', split_axis=1, concat_axis=0, tiled=True)  95.9 us
    dot_general x1, matrix products, middle(): jnp.einsum('nm,mkc->nkc', second_inverse, gated, preferred_element_type=j...  24 us
    all_to_all x1, local copies, waits for them, and re-layouts, per_device(): lax.all_to_all(first, 'seq', split_axis=1, concat_axis=0, tiled=True)  15.2 us
    convert_element_type x1, local copies, waits for them, and re-layouts, first_section(): (result * twiddle.astype(jnp.float32)[:, :, None]).astype(jnp.bfloat16)  12.6 us
    unnamed x13, local copies, waits for them, and re-layouts  12.3 us
    convert_element_type x1, local copies, waits for them, and re-layouts, middle(): return (back * twiddle.astype(jnp.float32)[:, :, None]).astype(jnp.bfloat16)  12.2 us
    all_to_all x1, starting transfers between devices, per_device(): lax.all_to_all(first, 'seq', split_axis=1, concat_axis=0, tiled=True)  11 us
  transfers between devices with their start and end apart: 1, of which 1 were waited for; matrix products, arithmetic and copies ran while one was open for 4% of the time, Pallas kernels for 0%

commit v1 on v0

v1 whole, which is shorter than its diff:
```python
import functools

import jax
import jax.numpy as jnp
from jax import lax
from jax.experimental import pallas as pl
from jax.experimental.pallas import tpu as pltpu
from jax.sharding import PartitionSpec as P

CHUNKS = 2
VMEM_LIMIT = 56 * 1024 * 1024


def params():
    return pltpu.CompilerParams(
        dimension_semantics=("arbitrary",), vmem_limit_bytes=VMEM_LIMIT
    )


def first_kernel(p_block, x_ref, inv_ref, gain_ref, factor_ref, tw_ref, out_ref, held):
    step = pl.program_id(0)
    order = factor_ref.shape[0]

    @pl.when(step < p_block)
    def _():
        scaled = (factor_ref[...] * inv_ref[0]).astype(jnp.bfloat16)
        result = jnp.dot(scaled, x_ref[...], preferred_element_type=jnp.float32)
        result = result * tw_ref[0] * gain_ref[...]
        for part in range(held.shape[0]):
            held[part, pl.ds(step, order, stride=p_block), :] = result[
                :, part * 128 : (part + 1) * 128
            ]

    @pl.when(step >= p_block)
    def _():
        rows = out_ref.shape[0]
        base = pl.multiple_of((step - p_block) * rows, rows)
        for part in range(held.shape[0]):
            out_ref[:, part * 128 : (part + 1) * 128] = held[
                part, pl.ds(base, rows), :
            ].astype(jnp.bfloat16)


def first_call(tokens, inv, gain, factor, tw, chunk, width):
    rows, _ = tokens.shape
    p_block, _, order = inv.shape
    parts = 8
    out_rows = rows // parts
    return pl.pallas_call(
        functools.partial(first_kernel, p_block),
        grid=(p_block + parts,),
        in_specs=[
            pl.BlockSpec((order, width), lambda i: (jnp.minimum(i, p_block - 1), chunk)),
            pl.BlockSpec((1, 1, order), lambda i: (jnp.minimum(i, p_block - 1), 0, 0)),
            pl.BlockSpec((1, width), lambda i: (0, chunk)),
            pl.BlockSpec((order, order), lambda i: (0, 0)),
            pl.BlockSpec((1, order, 1), lambda i: (jnp.minimum(i, p_block - 1), 0, 0)),
        ],
        out_specs=pl.BlockSpec((out_rows, width), lambda i: (jnp.maximum(i - p_block, 0), 0)),
        out_shape=jax.ShapeDtypeStruct((rows, width), jnp.bfloat16),
        scratch_shapes=[pltpu.VMEM((width // 128, rows, 128), jnp.float32)],
        compiler_params=params(),
        cost_estimate=pl.CostEstimate(
            flops=2 * rows * order * width, bytes_accessed=4 * rows * width, transcendentals=0
        ),
        name="first_section",
    )(tokens, inv, gain, factor, tw)


def middle_kernel(pairs, v_ref, pair_ref, gate_ref, inverse_ref, tw_ref, out_ref, held):
    step = pl.program_id(0)
    groups, _, width = v_ref.shape
    m_order = inverse_ref.shape[0]

    @pl.when(step < pairs)
    def _():
        values = v_ref[...].reshape(groups * 16, width)
        gated = jnp.dot(pair_ref[...], values, preferred_element_type=jnp.float32)
        for one in range(2):
            half = gated[one * m_order : (one + 1) * m_order]
            half = (half * gate_ref[one].astype(jnp.float32)).astype(jnp.bfloat16)
            back = jnp.dot(inverse_ref[...], half, preferred_element_type=jnp.float32)
            back = back * tw_ref[one]
            for part in range(held.shape[0]):
                held[part, pl.ds(2 * step + one, m_order, stride=2 * pairs), :] = back[
                    :, part * 128 : (part + 1) * 128
                ]

    @pl.when(step >= pairs)
    def _():
        rows = out_ref.shape[0]
        base = pl.multiple_of((step - pairs) * rows, rows)
        for part in range(held.shape[0]):
            out_ref[:, part * 128 : (part + 1) * 128] = held[
                part, pl.ds(base, rows), :
            ].astype(jnp.bfloat16)


def middle_call(values, pair, gate, inverse, tw, chunk):
    groups, depth, width = values.shape
    pairs = depth // 16
    m_order = inverse.shape[0]
    rows = groups * depth
    parts = 8
    last = pairs - 1
    return pl.pallas_call(
        functools.partial(middle_kernel, pairs),
        grid=(pairs + parts,),
        in_specs=[
            pl.BlockSpec((groups, 16, width), lambda i: (0, jnp.minimum(i, last), 0)),
            pl.BlockSpec((2 * m_order, 2 * m_order), lambda i: (0, 0)),
            pl.BlockSpec((2, m_order, width), lambda i: (jnp.minimum(i, last), 0, chunk)),
            pl.BlockSpec((m_order, m_order), lambda i: (0, 0)),
            pl.BlockSpec((2, m_order, 1), lambda i: (jnp.minimum(i, last), 0, 0)),
        ],
        out_specs=pl.BlockSpec((rows // parts, width), lambda i: (jnp.maximum(i - pairs, 0), 0)),
        out_shape=jax.ShapeDtypeStruct((rows, width), jnp.bfloat16),
        scratch_shapes=[pltpu.VMEM((width // 128, rows, 128), jnp.float32)],
        compiler_params=params(),
        cost_estimate=pl.CostEstimate(
            flops=6 * rows * m_order * width, bytes_accessed=6 * rows * width, transcendentals=0
        ),
        name="middle_section",
    )(values, pair, gate, inverse, tw)


def last_kernel(v_ref, factor_ref, *rest):
    out_ref = rest[-1]
    groups, depth, width = v_ref.shape
    values = v_ref[...].reshape(groups * depth, width)
    out_ref[...] = jnp.dot(factor_ref[...], values, preferred_element_type=jnp.float32).astype(
        jnp.bfloat16
    )


def last_call(values, factor, so_far, chunk, full_width):
    groups, depth, width = values.shape
    order = factor.shape[0]
    per = order // groups
    blocks = depth // per
    in_specs = [
        pl.BlockSpec((groups, per, width), lambda i: (0, i, 0)),
        pl.BlockSpec((order, order), lambda i: (0, 0)),
    ]
    operands = [values, factor]
    aliases = {}
    if so_far is not None:
        in_specs.append(pl.BlockSpec(memory_space=pl.ANY))
        operands.append(so_far)
        aliases = {2: 0}
    return pl.pallas_call(
        last_kernel,
        grid=(blocks,),
        in_specs=in_specs,
        out_specs=pl.BlockSpec((order, width), lambda i: (i, chunk)),
        out_shape=jax.ShapeDtypeStruct((blocks * order, full_width), jnp.bfloat16),
        input_output_aliases=aliases,
        compiler_params=params(),
        cost_estimate=pl.CostEstimate(
            flops=2 * blocks * order * order * width,
            bytes_accessed=4 * blocks * order * width,
            transcendentals=0,
        ),
        name="last_section",
    )(*operands)


def per_device(
    tokens,
    norm_gain,
    first_factor,
    twiddle_in,
    second_factor,
    kernel_gate,
    second_inverse,
    twiddle_out,
    first_inverse,
):
    f32 = jnp.float32
    seq_count = lax.axis_size("seq")
    rows_dev, width_dev = tokens.shape
    q_order = first_factor.shape[0]
    p_order = second_factor.shape[0]
    p_block = p_order // seq_count
    k_block = q_order // seq_count
    width = width_dev // CHUNKS

    widened = tokens.astype(f32)
    square = lax.psum(jnp.sum(widened * widened, axis=1), "chan")
    inverse_rms = lax.rsqrt(square / (width_dev * lax.axis_size("chan")) + 1e-05)
    inverse_rms = inverse_rms.reshape(p_block, 1, q_order)

    gain = norm_gain.astype(f32).reshape(1, width_dev)
    factor = first_factor.astype(f32)
    tw_in = twiddle_in.astype(f32)[:, :, None]
    tw_out = twiddle_out.astype(f32).T[:, :, None]
    gate = kernel_gate.transpose(1, 0, 2)
    split = second_factor.reshape(p_order, seq_count, 1, p_block)
    none = jnp.zeros_like(split)
    pair = jnp.stack(
        [jnp.concatenate([split, none], axis=2), jnp.concatenate([none, split], axis=2)]
    ).reshape(2 * p_order, 2 * p_order)

    sent = [
        first_call(tokens, inverse_rms, gain, factor, tw_in, chunk, width)
        for chunk in range(CHUNKS)
    ]
    shape = (seq_count, rows_dev // seq_count, width)
    columns = [
        lax.all_to_all(one.reshape(shape), "seq", split_axis=0, concat_axis=0, tiled=True)
        for one in sent
    ]
    backs = [
        middle_call(one, pair, gate, second_inverse, tw_out, chunk)
        for chunk, one in enumerate(columns)
    ]
    returned = [
        lax.all_to_all(one.reshape(shape), "seq", split_axis=0, concat_axis=0, tiled=True)
        for one in backs
    ]
    out = None
    for chunk, one in enumerate(returned):
        out = last_call(one, first_inverse, out, chunk, width_dev)
    return out


def solution(mesh):
    return jax.shard_map(
        per_device,
        mesh=mesh,
        in_specs=(
            P("seq", "chan"),
            P("chan"),
            P(),
            P("seq", None),
            P(),
            P(None, "seq", "chan"),
            P(),
            P(None, "seq"),
            P(),
        ),
        out_specs=P("seq", "chan"),
        check_vma=False,
    )
```

time: 348 us -> 305 us (0.88)
  the two profiles are of different devices: /device:TPU:1 before, /device:TPU:12 now
where the time goes in v1:
time: 305 us; the launch traced here: 303 us
  waiting for transfers between devices  163 us (53%)
  Pallas kernels  69.7 us (23%)
  starting transfers between devices  34.6 us (11%)
  local copies, waits for them, and re-layouts  17.3 us (6%)
  blocking collectives  10.1 us (3%)
  other arithmetic  8.9 us (3%)
    all_to_all x4, waiting for transfers between devices, per_device(): lax.all_to_all(one.reshape(shape), 'seq', split_axis=0, concat_axis=0, ti...  163 us
    all_to_all x4, starting transfers between devices, per_device(): lax.all_to_all(one.reshape(shape), 'seq', split_axis=0, concat_axis=0, ti...  34.6 us
    pallas_call x2, Pallas kernels, middle_call(): pl.pallas_call(functools.partial(middle_kernel, pairs), grid=(pairs + par...  29.5 us
    pallas_call x2, Pallas kernels, first_call(): pl.pallas_call(functools.partial(first_kernel, p_block), grid=(p_block +...  23.8 us
    pallas_call x2, Pallas kernels, last_call(): pl.pallas_call(last_kernel, grid=(blocks,), in_specs=in_specs, out_specs=...  16.4 us
    unnamed x9, local copies, waits for them, and re-layouts  11.7 us
    psum x1, blocking collectives, per_device(): square = lax.psum(jnp.sum(widened * widened, axis=1), 'chan')  10.1 us
  transfers between devices with their start and end apart: 4, of which 4 were waited for; matrix products, arithmetic and copies ran while one was open for 5% of the time, Pallas kernels for 16%

profile of v1, /device:TPU:12, one launch (start us, length us, event | category | flops | bytes accessed | tf_op | source)
XLA Modules:
  0.0 303.4 jit_solution(14857065455170204938)
XLA Ops:
  0.0 1.3 reshape.35
  1.3 0.7 bitcast_convert_fusion
  2.0 5.1 %multiply_reduce_fusion = f32[4096]{0:T(1024)S(1)} fusion(bf16[4096,1024]{1,0:T(8,128)(2,1)} %x_ref.3), kind=kLoop, calls=%fused_computation | loop fusion | flops 12578816 | bytes 8404992 | tf_op jit(solution)/shard_map/reduce_sum | solution.py:189
  7.1 10.1 %psum.7 = f32[4096]{0:T(1024)S(1)} all-reduce(f32[4096]{0:T(1024)S(1)} %multiply_reduce_fusion), channel_id=1, replica_groups=mesh['seq'=32,'chan'=4] {'chan'}, use_global_device_ids=true, to_apply=%region_1.0 | all-reduce | flops 4096 | bytes 32768 | tf_op jit(solution)/shard_map/psum | solution.py:189
  17.3 0.6 add_rsqrt_fusion
  17.9 1.1 convert_element_type.10.factor_ref
  19.0 2.0 copy.14.tw_ref
  21.0 11.8 %first_section.3 = bf16[4096,512]{1,0:T(8,128)(2,1)} custom-call(bf16[4096,1024]{1,0:T(8,128)(2,1)} %x_ref.3, f32[8,1,512]{2,1,0:T(1,128)} %bitcast.35, f32[1,1024]{1,0:T(1,128)} %bitcast.37, f32[512,512]{1,0:T(8,128)} %convert_element_type.10.factor_ref, f32[8,512,1]{2,1,0:T(8,128)} %copy.14.tw_ref), custom_call_target="tpu_custom_call" | custom-call | flops 2147483648 | bytes 8388608 | tf_op jit(solution)/shard_map/first_section/pallas_call | solution.py:49
  32.8 10.5 %all-to-all-start.2 = ((bf16[32,128,512]{2,1,0:T(8,128)(2,1)}), bf16[32,128,512]{2,1,0:T(8,128)(2,1)}, u32[]{:S(2)}, u32[]{:S(2)}) async-start(bf16[32,128,512]{2,1,0:T(8,128)(2,1)} %bitcast.31), calls=%async_computation.2 | async-start | bytes 8388608 | tf_op jit(solution)/shard_map/all_to_all | solution.py:210
  43.4 12.0 %first_section.2 = bf16[4096,512]{1,0:T(8,128)(2,1)} custom-call(bf16[4096,1024]{1,0:T(8,128)(2,1)} %x_ref.3, f32[8,1,512]{2,1,0:T(1,128)} %bitcast.36, f32[1,1024]{1,0:T(1,128)} %bitcast.38, f32[512,512]{1,0:T(8,128)} %convert_element_type.10.factor_ref, f32[8,512,1]{2,1,0:T(8,128)} %copy.14.tw_ref), custom_call_target="tpu_custom_call" | custom-call | flops 2147483648 | bytes 8388608 | tf_op jit(solution)/shard_map/first_section/pallas_call | solution.py:49
  55.3 42.2 %all-to-all-done.2.v_ref = bf16[32,128,512]{2,1,0:T(8,128)(2,1)} async-done(((bf16[32,128,512]{2,1,0:T(8,128)(2,1)}), bf16[32,128,512]{2,1,0:T(8,128)(2,1)}, u32[]{:S(2)}, u32[]{:S(2)}) %all-to-all-start.2) | async-done | bytes 4194336 | tf_op jit(solution)/shard_map/all_to_all | solution.py:210
  97.5 10.3 %all-to-all-start = ((bf16[32,128,512]{2,1,0:T(8,128)(2,1)}), bf16[32,128,512]{2,1,0:T(8,128)(2,1)}, u32[]{:S(2)}, u32[]{:S(2)}) async-start(bf16[32,128,512]{2,1,0:T(8,128)(2,1)} %bitcast.28), calls=%async_computation | async-start | bytes 8388608 | tf_op jit(solution)/shard_map/all_to_all | solution.py:210
  108.7 1.0 copy.18.pair_ref
  109.7 2.0 copy.19.tw_ref
  111.7 11.5 %copy.25 = bf16[256,16,1024]{2,0,1:T(8,128)(2,1)} copy(bf16[256,16,1024]{2,1,0:T(8,128)(2,1)} %param.14) | data formatting | bytes 16777216 | tf_op args[5]
  123.2 14.7 %middle_section.3 = bf16[4096,512]{1,0:T(8,128)(2,1)} custom-call(bf16[32,128,512]{2,1,0:T(8,128)(2,1)} %all-to-all-done.2.v_ref, bf16[512,512]{1,0:T(8,128)(2,1)} %copy.18.pair_ref, bf16[16,256,1024]{2,1,0:T(8,128)(2,1)} %bitcast.26, bf16[256,256]{1,0:T(8,128)(2,1)} %inverse_ref.3, f32[16,256,1]{2,1,0:T(8,128)} %copy.19.tw_ref), custom_call_target="tpu_custom_call" | custom-call | flops 3221225472 | bytes 12582912 | tf_op jit(solution)/shard_map/middle_section/pallas_call | solution.py:106
  137.9 33.0 %all-to-all-done.v_ref = bf16[32,128,512]{2,1,0:T(8,128)(2,1)} async-done(((bf16[32,128,512]{2,1,0:T(8,128)(2,1)}), bf16[32,128,512]{2,1,0:T(8,128)(2,1)}, u32[]{:S(2)}, u32[]{:S(2)}) %all-to-all-start) | async-done | bytes 4194336 | tf_op jit(solution)/shard_map/all_to_all | solution.py:210
  170.9 5.5 %all-to-all-start.3 = ((bf16[32,128,512]{2,1,0:T(8,128)(2,1)}), bf16[32,128,512]{2,1,0:T(8,128)(2,1)}, u32[]{:S(2)}, u32[]{:S(2)}) async-start(bf16[32,128,512]{2,1,0:T(8,128)(2,1)} %bitcast.29), calls=%async_computation.3 | async-start | bytes 8388608 | tf_op jit(solution)/shard_map/all_to_all | solution.py:218
  176.4 14.8 %middle_section.2 = bf16[4096,512]{1,0:T(8,128)(2,1)} custom-call(bf16[32,128,512]{2,1,0:T(8,128)(2,1)} %all-to-all-done.v_ref, bf16[512,512]{1,0:T(8,128)(2,1)} %copy.18.pair_ref, bf16[16,256,1024]{2,1,0:T(8,128)(2,1)} %bitcast.27, bf16[256,256]{1,0:T(8,128)(2,1)} %inverse_ref.3, f32[16,256,1]{2,1,0:T(8,128)} %copy.19.tw_ref), custom_call_target="tpu_custom_call" | custom-call | flops 3221225472 | bytes 12582912 | tf_op jit(solution)/shard_map/middle_section/pallas_call | solution.py:106
  191.2 42.0 %all-to-all-done.3.v_ref = bf16[32,128,512]{2,1,0:T(8,128)(2,1)} async-done(((bf16[32,128,512]{2,1,0:T(8,128)(2,1)}), bf16[32,128,512]{2,1,0:T(8,128)(2,1)}, u32[]{:S(2)}, u32[]{:S(2)}) %all-to-all-start.3) | async-done | bytes 4194336 | tf_op jit(solution)/shard_map/all_to_all | solution.py:218
  233.2 8.2 %all-to-all-start.1 = ((bf16[32,128,512]{2,1,0:T(8,128)(2,1)}), bf16[32,128,512]{2,1,0:T(8,128)(2,1)}, u32[]{:S(2)}, u32[]{:S(2)}) async-start(bf16[32,128,512]{2,1,0:T(8,128)(2,1)} %bitcast.30), calls=%async_computation.1 | async-start | bytes 8388608 | tf_op jit(solution)/shard_map/all_to_all | solution.py:218
  241.5 8.2 %last_section.2.rest_0_ = bf16[4096,1024]{1,0:T(8,128)(2,1)} custom-call(bf16[32,128,512]{2,1,0:T(8,128)(2,1)} %all-to-all-done.3.v_ref, bf16[512,512]{1,0:T(8,128)(2,1)} %factor_ref.3), custom_call_target="tpu_custom_call" | custom-call | flops 2147483648 | bytes 8388608 | tf_op jit(solution)/shard_map/last_section/pallas_call | solution.py:151
  249.7 45.5 %all-to-all-done.1.v_ref = bf16[32,128,512]{2,1,0:T(8,128)(2,1)} async-done(((bf16[32,128,512]{2,1,0:T(8,128)(2,1)}), bf16[32,128,512]{2,1,0:T(8,128)(2,1)}, u32[]{:S(2)}, u32[]{:S(2)}) %all-to-all-start.1) | async-done | bytes 4194336 | tf_op jit(solution)/shard_map/all_to_all | solution.py:218
  295.2 8.2 %last_section.3 = bf16[4096,1024]{1,0:T(8,128)(2,1)} custom-call(bf16[32,128,512]{2,1,0:T(8,128)(2,1)} %all-to-all-done.1.v_ref, bf16[512,512]{1,0:T(8,128)(2,1)} %factor_ref.3, bf16[4096,1024]{1,0:T(8,128)(2,1)} %last_section.2.rest_0_), custom_call_target="tpu_custom_call", output_to_operand_aliasing={{}: (2, {})} | custom-call | flops 2147483648 | bytes 8388608 | tf_op jit(solution)/shard_map/last_section/pallas_call | solution.py:151
  (12 shorter events, 0.8 us)
Async XLA Ops:
  2.0 15.9 %copy-start = (bf16[512,512]{1,0:T(8,128)(2,1)S(1)}, bf16[512,512]{1,0:T(8,128)(2,1)}, u32[]{:S(2)}) copy-start(bf16[512,512]{1,0:T(8,128)(2,1)} %param.11) | copy-start | bytes 1572868
  32.8 64.7 %all-to-all-start.2 = ((bf16[32,128,512]{2,1,0:T(8,128)(2,1)}), bf16[32,128,512]{2,1,0:T(8,128)(2,1)}, u32[]{:S(2)}, u32[]{:S(2)}) async-start(bf16[32,128,512]{2,1,0:T(8,128)(2,1)} %bitcast.31), calls=%async_computation.2 | async-start | bytes 8388608 | tf_op jit(solution)/shard_map/all_to_all | solution.py:210
  97.5 10.3 %copy-start.1 = (bf16[256,256]{1,0:T(8,128)(2,1)S(1)}, bf16[256,256]{1,0:T(8,128)(2,1)}, u32[]{:S(2)}) copy-start(bf16[256,256]{1,0:T(8,128)(2,1)} %param.13) | copy-start | bytes 393220
  97.5 73.4 %all-to-all-start = ((bf16[32,128,512]{2,1,0:T(8,128)(2,1)}), bf16[32,128,512]{2,1,0:T(8,128)(2,1)}, u32[]{:S(2)}, u32[]{:S(2)}) async-start(bf16[32,128,512]{2,1,0:T(8,128)(2,1)} %bitcast.28), calls=%async_computation | async-start | bytes 8388608 | tf_op jit(solution)/shard_map/all_to_all | solution.py:210
  107.8 1.9 copy-start.2
  170.9 62.3 %all-to-all-start.3 = ((bf16[32,128,512]{2,1,0:T(8,128)(2,1)}), bf16[32,128,512]{2,1,0:T(8,128)(2,1)}, u32[]{:S(2)}, u32[]{:S(2)}) async-start(bf16[32,128,512]{2,1,0:T(8,128)(2,1)} %bitcast.29), calls=%async_computation.3 | async-start | bytes 8388608 | tf_op jit(solution)/shard_map/all_to_all | solution.py:218
  233.2 61.9 %all-to-all-start.1 = ((bf16[32,128,512]{2,1,0:T(8,128)(2,1)}), bf16[32,128,512]{2,1,0:T(8,128)(2,1)}, u32[]{:S(2)}, u32[]{:S(2)}) async-start(bf16[32,128,512]{2,1,0:T(8,128)(2,1)} %bitcast.30), calls=%async_computation.1 | async-start | bytes 8388608 | tf_op jit(solution)/shard_map/all_to_all | solution.py:218

commit v2 on v0

v2 whole, which is shorter than its diff:
```python
import jax
import jax.numpy as jnp
from jax import lax
from jax.experimental import pallas as pl
from jax.experimental.pallas import tpu as pltpu
from jax.sharding import PartitionSpec as P

LANES = 128
TILE = 256
VMEM_LIMIT = 48 * 1024 * 1024


def params():
    return pltpu.CompilerParams(
        dimension_semantics=("arbitrary",), vmem_limit_bytes=VMEM_LIMIT
    )


def first_kernel(x_ref, inv_ref, gain_ref, factor_ref, tw_ref, out_ref, tables, held):
    p_block, order, _ = tables.shape
    parts = held.shape[0]

    @pl.when(pl.program_id(0) == 0)
    def _():
        factor = factor_ref[...].astype(jnp.float32)
        for p in range(p_block):
            scaled = factor * inv_ref[p : p + 1, :] * tw_ref[:, p : p + 1]
            tables[p] = scaled.astype(jnp.bfloat16)

    for p in range(p_block):
        result = jnp.dot(
            tables[p], x_ref[p * order : (p + 1) * order, :], preferred_element_type=jnp.float32
        )
        result = result * gain_ref[...].astype(jnp.float32)
        for part in range(parts):
            held[part, pl.ds(p, order, stride=p_block), :] = result[
                :, part * LANES : (part + 1) * LANES
            ]
    for part in range(parts):
        out_ref[:, part * LANES : (part + 1) * LANES] = held[part].astype(jnp.bfloat16)


def first_call(tokens, inv, gain, factor, tw):
    rows, width = tokens.shape
    p_block, order = inv.shape
    return pl.pallas_call(
        first_kernel,
        grid=(width // TILE,),
        in_specs=[
            pl.BlockSpec((rows, TILE), lambda i: (0, i)),
            pl.BlockSpec((p_block, order), lambda i: (0, 0)),
            pl.BlockSpec((1, TILE), lambda i: (0, i)),
            pl.BlockSpec((order, order), lambda i: (0, 0)),
            pl.BlockSpec((order, p_block), lambda i: (0, 0)),
        ],
        out_specs=pl.BlockSpec((rows, TILE), lambda i: (0, i)),
        out_shape=jax.ShapeDtypeStruct((rows, width), jnp.bfloat16),
        scratch_shapes=[
            pltpu.VMEM((p_block, order, order), jnp.bfloat16),
            pltpu.VMEM((TILE // LANES, rows, LANES), jnp.float32),
        ],
        compiler_params=params(),
        cost_estimate=pl.CostEstimate(
            flops=2 * rows * order * width, bytes_accessed=4 * rows * width, transcendentals=0
        ),
        name="first_section",
    )(tokens, inv, gain, factor, tw)


def middle_kernel(v_ref, second_ref, gate_ref, inverse_ref, tw_ref, out_ref, tables, held, gates):
    groups, _, tile = v_ref.shape
    k_block, m_order, _ = tables.shape
    parts = held.shape[0]
    f32 = jnp.float32

    @pl.when(pl.program_id(0) == 0)
    def _():
        inverse = inverse_ref[...].astype(f32)
        for k in range(k_block):
            tables[k] = (inverse * tw_ref[:, k : k + 1]).astype(jnp.bfloat16)

    gate = gate_ref[...].reshape(m_order * k_block, tile)
    for part in range(parts):
        gates[part] = gate[:, part * LANES : (part + 1) * LANES].astype(f32)

    for pair in range(k_block // 2):
        both = v_ref[:, pair * 16 : (pair + 1) * 16, :].astype(f32).reshape(groups, 2, 8, tile)
        for one in range(2):
            k = 2 * pair + one
            values = both[:, one].reshape(groups * 8, tile).astype(jnp.bfloat16)
            gated = jnp.dot(second_ref[...], values, preferred_element_type=f32)
            here = jnp.concatenate(
                [gates[part, pl.ds(k, m_order, stride=k_block), :] for part in range(parts)], axis=1
            )
            gated = (gated * here).astype(jnp.bfloat16)
            back = jnp.dot(tables[k], gated, preferred_element_type=f32)
            for part in range(parts):
                held[part, pl.ds(k, m_order, stride=k_block), :] = back[
                    :, part * LANES : (part + 1) * LANES
                ]
    for part in range(parts):
        out_ref[:, part * LANES : (part + 1) * LANES] = held[part].astype(jnp.bfloat16)


def middle_call(values, second, gate, inverse, tw):
    groups, depth, width = values.shape
    m_order, k_block = tw.shape
    rows = groups * depth
    return pl.pallas_call(
        middle_kernel,
        grid=(width // TILE,),
        in_specs=[
            pl.BlockSpec((groups, depth, TILE), lambda i: (0, 0, i)),
            pl.BlockSpec((m_order, m_order), lambda i: (0, 0)),
            pl.BlockSpec((m_order, k_block, TILE), lambda i: (0, 0, i)),
            pl.BlockSpec((m_order, m_order), lambda i: (0, 0)),
            pl.BlockSpec((m_order, k_block), lambda i: (0, 0)),
        ],
        out_specs=pl.BlockSpec((rows, TILE), lambda i: (0, i)),
        out_shape=jax.ShapeDtypeStruct((rows, width), jnp.bfloat16),
        scratch_shapes=[
            pltpu.VMEM((k_block, m_order, m_order), jnp.bfloat16),
            pltpu.VMEM((TILE // LANES, rows, LANES), jnp.float32),
            pltpu.VMEM((TILE // LANES, rows, LANES), jnp.float32),
        ],
        compiler_params=params(),
        cost_estimate=pl.CostEstimate(
            flops=4 * rows * m_order * width, bytes_accessed=6 * rows * width, transcendentals=0
        ),
        name="middle_section",
    )(values, second, gate, inverse, tw)


def last_kernel(per, v_ref, factor_ref, out_ref):
    groups, depth, width = v_ref.shape
    order = factor_ref.shape[0]
    for part in range(depth // per):
        values = v_ref[:, part * per : (part + 1) * per, :].reshape(order, width)
        out_ref[part * order : (part + 1) * order, :] = jnp.dot(
            factor_ref[...], values, preferred_element_type=jnp.float32
        ).astype(jnp.bfloat16)


def last_call(values, factor):
    groups, depth, width = values.shape
    order = factor.shape[0]
    per = order // groups
    steps = 2
    rows = groups * depth
    return pl.pallas_call(
        lambda *refs: last_kernel(per, *refs),
        grid=(steps,),
        in_specs=[
            pl.BlockSpec((groups, depth // steps, width), lambda i: (0, i, 0)),
            pl.BlockSpec((order, order), lambda i: (0, 0)),
        ],
        out_specs=pl.BlockSpec((rows // steps, width), lambda i: (i, 0)),
        out_shape=jax.ShapeDtypeStruct((rows, width), jnp.bfloat16),
        compiler_params=params(),
        cost_estimate=pl.CostEstimate(
            flops=2 * rows * order * width, bytes_accessed=4 * rows * width, transcendentals=0
        ),
        name="last_section",
    )(values, factor)


def chan_sum(part):
    count = lax.axis_size("chan")
    total = part
    for shift in range(1, count):
        pairs = [(i, (i + shift) % count) for i in range(count)]
        total = total + lax.ppermute(part, "chan", pairs)
    return total


def per_device(
    tokens,
    norm_gain,
    first_factor,
    twiddle_in,
    second_factor,
    kernel_gate,
    second_inverse,
    twiddle_out,
    first_inverse,
):
    f32 = jnp.float32
    seq_count = lax.axis_size("seq")
    rows_dev, width_dev = tokens.shape
    q_order = first_factor.shape[0]
    p_block = rows_dev // q_order

    widened = tokens.reshape(p_block, q_order, width_dev).astype(f32)
    square = chan_sum(jnp.sum(widened * widened, axis=2))
    inverse_rms = lax.rsqrt(square / (width_dev * lax.axis_size("chan")) + 1e-05)

    sent = first_call(
        tokens,
        inverse_rms,
        norm_gain.reshape(1, width_dev),
        first_factor,
        twiddle_in.T.astype(f32),
    )
    shape = (seq_count, rows_dev // seq_count, width_dev)
    sent, tw_out = lax.optimization_barrier((sent.reshape(shape), twiddle_out.astype(f32)))
    columns = lax.all_to_all(sent, "seq", split_axis=0, concat_axis=0, tiled=True)
    back = middle_call(columns, second_factor, kernel_gate, second_inverse, tw_out)
    returned = lax.all_to_all(back.reshape(shape), "seq", split_axis=0, concat_axis=0, tiled=True)
    return last_call(returned, first_inverse)


def solution(mesh):
    return jax.shard_map(
        per_device,
        mesh=mesh,
        in_specs=(
            P("seq", "chan"),
            P("chan"),
            P(),
            P("seq", None),
            P(),
            P(None, "seq", "chan"),
            P(),
            P(None, "seq"),
            P(),
        ),
        out_specs=P("seq", "chan"),
        check_vma=False,
    )
```

time: 348 us -> 259 us (0.74)
  waiting for transfers between devices: 95.9 us -> 0.55 us
  blocking collectives: 123 us -> 208 us
  local copies, waits for them, and re-layouts: 60.9 us -> 0.29 us
  matrix products: 41.1 us -> 0 us
  Pallas kernels: 0 us -> 38.7 us
  starting transfers between devices: 11 us -> 4.22 us
  other arithmetic: 11.6 us -> 5.17 us
    all_to_all x1 -> x0, waiting for transfers between devices: 95.9 us -> none  [per_device(): lax.all_to_all(first, 'seq', split_axis=1, concat_axis=0, tiled=True)]
    all_to_all x1 -> x2, blocking collectives: 113 us -> 208 us  [the longest x1 105 us: per_device(): lax.all_to_all(sent, 'seq', split_axis=0, concat_axis=0, tiled=True)]
    dot_general x3 -> x0, matrix products: 41.1 us -> none  [the longest x1 24 us: middle(): jnp.einsum('nm,mkc->nkc', second_inverse, gated, preferred_element_type=j...]
    pallas_call x0 -> x3, Pallas kernels: none -> 38.7 us  [the longest x1 18.5 us: middle_call(): pl.pallas_call(middle_kernel, grid=(width // TILE,), in_specs=[pl.BlockSp...]
    convert_element_type x2 -> x1, local copies, waits for them, and re-layouts: 24.9 us -> 0.13 us  [per_device(): twiddle_in.T.astype(f32)]
    all_to_all x2 -> x0, local copies, waits for them, and re-layouts: 23.8 us -> none  [the longest x1 15.2 us: per_device(): lax.all_to_all(first, 'seq', split_axis=1, concat_axis=0, tiled=True)]
    unnamed x13 -> x15, local copies, waits for them, and re-layouts: 12.3 us -> 0.15 us
    all_to_all x1 -> x0, starting transfers between devices: 11 us -> none  [per_device(): lax.all_to_all(first, 'seq', split_axis=1, concat_axis=0, tiled=True)]
  transfers between devices with their start and end apart: 1 -> 3, of which waited for: 1 -> 1; matrix products, arithmetic and copies ran while one was open for 4% -> 0% of each run, Pallas kernels for 0% -> 0%
where the time goes in v2:
time: 259 us; the launch traced here: 257 us
  blocking collectives  208 us (80%)
  Pallas kernels  38.7 us (15%)
  other arithmetic  5.17 us (2%)
  starting transfers between devices  4.22 us (2%)
    all_to_all x1, blocking collectives, per_device(): lax.all_to_all(sent, 'seq', split_axis=0, concat_axis=0, tiled=True)  105 us
    all_to_all x1, blocking collectives, per_device(): lax.all_to_all(back.reshape(shape), 'seq', split_axis=0, concat_axis=0, t...  103 us
    pallas_call x1, Pallas kernels, middle_call(): pl.pallas_call(middle_kernel, grid=(width // TILE,), in_specs=[pl.BlockSp...  18.5 us
    pallas_call x1, Pallas kernels, first_call(): pl.pallas_call(first_kernel, grid=(width // TILE,), in_specs=[pl.BlockSpe...  11.3 us
    pallas_call x1, Pallas kernels, last_call(): pl.pallas_call(lambda *refs: last_kernel(per, *refs), grid=(steps,), in_s...  8.92 us
  transfers between devices with their start and end apart: 3, of which 1 were waited for; matrix products, arithmetic and copies ran while one was open for 0% of the time, Pallas kernels for 0%

profile of v2, /device:TPU:1, one launch (start us, length us, event | category | flops | bytes accessed | tf_op | source)
XLA Modules:
  0.0 257.3 jit_solution(7152655355569161999)
XLA Ops:
  0.0 0.0 copy-start.6
  0.0 0.0 copy-start.4
  0.0 0.0 copy-start
  0.0 5.1 %multiply_reduce_fusion = f32[4096]{0:T(1024)S(1)} fusion(bf16[4096,1024]{1,0:T(8,128)(2,1)} %x_ref.1), kind=kLoop, calls=%fused_computation | loop fusion | flops 12578816 | bytes 8404992 | tf_op jit(solution)/shard_map/reduce_sum | solution.py:194
  5.2 1.5 collective-permute-start.2
  6.7 1.4 collective-permute-start.1
  8.1 1.3 collective-permute-start
  9.4 0.0 copy-done.6
  9.4 0.0 copy-done.4
  9.4 0.1 copy.11
  9.6 0.0 copy-done.5
  9.6 0.1 copy.10
  9.7 0.0 collective-permute-done.2
  9.7 0.0 collective-permute-done.1
  9.7 0.5 collective-permute-done
  10.3 0.0 copy-done
  10.3 11.3 %first_section.1 = bf16[4096,1024]{1,0:T(8,128)(2,1)} custom-call(bf16[4096,1024]{1,0:T(8,128)(2,1)} %x_ref.1, f32[8,512]{1,0:T(8,128)S(1)} %add_rsqrt_fusion.inv_ref, bf16[1,1024]{1,0:T(2,128)(2,1)S(1)} %reshape.11.gain_ref, bf16[512,512]{1,0:T(8,128)(2,1)S(1)} %copy-done, f32[512,8]{1,0:T(8,128)S(1)} %bitcast.3), custom_call_target="tpu_custom_call" | custom-call | flops 4294967296 | bytes 16777216 | tf_op jit(solution)/shard_map/first_section/pallas_call | solution.py:46
  21.6 105.0 %all_to_all.10.v_ref = bf16[32,128,1024]{2,1,0:T(8,128)(2,1)} all-to-all(bf16[32,128,1024]{2,1,0:T(8,128)(2,1)} %bitcast.5), channel_id=1, replica_groups=mesh['seq'=32,'chan'=4] {'seq'}, dimensions={0} | all-to-all | bytes 16777216 | tf_op jit(solution)/shard_map/all_to_all | solution.py:206
  126.6 0.0 copy-done.2
  126.7 0.0 copy-done.3
  126.7 18.5 %middle_section.1 = bf16[4096,1024]{1,0:T(8,128)(2,1)} custom-call(bf16[32,128,1024]{2,1,0:T(8,128)(2,1)} %all_to_all.10.v_ref, bf16[256,256]{1,0:T(8,128)(2,1)S(1)} %copy-done.2, bf16[256,16,1024]{2,1,0:T(8,128)(2,1)} %gate_ref.1, bf16[256,256]{1,0:T(8,128)(2,1)S(1)} %copy-done.3, f32[256,16]{1,0:T(8,128)S(1)} %convert_element_type.15.tw_ref), custom_call_target="tpu_custom_call" | custom-call | flops 4294967296 | bytes 25165824 | tf_op jit(solution)/shard_map/middle_section/pallas_call | solution.py:109
  145.1 103.3 %all_to_all.11.refs_0_ = bf16[32,128,1024]{2,1,0:T(8,128)(2,1)} all-to-all(bf16[32,128,1024]{2,1,0:T(8,128)(2,1)} %bitcast.4), channel_id=1, replica_groups=mesh['seq'=32,'chan'=4] {'seq'}, dimensions={0} | all-to-all | bytes 16777216 | tf_op jit(solution)/shard_map/all_to_all | solution.py:208
  248.4 0.0 copy-done.1
  248.4 8.9 %last_section.1 = bf16[4096,1024]{1,0:T(8,128)(2,1)} custom-call(bf16[32,128,1024]{2,1,0:T(8,128)(2,1)} %all_to_all.11.refs_0_, bf16[512,512]{1,0:T(8,128)(2,1)S(1)} %copy-done.1), custom_call_target="tpu_custom_call" | custom-call | flops 4294967296 | bytes 16777216 | tf_op jit(solution)/shard_map/last_section/pallas_call | solution.py:150
  (8 shorter events, 0.0 us)
Async XLA Ops:
  0.0 9.4 %copy-start.6 = (bf16[1024]{0:T(1024)(128)(2,1)S(1)}, bf16[1024]{0:T(1024)(128)(2,1)}, u32[]{:S(2)}) copy-start(bf16[1024]{0:T(1024)(128)(2,1)} %param.10) | copy-start | bytes 6148
  0.0 9.4 %copy-start.4 = (bf16[256,16]{0,1:T(8,128)(2,1)S(1)}, bf16[256,16]{0,1:T(8,128)(2,1)}, u32[]{:S(2)}) copy-start(bf16[256,16]{0,1:T(8,128)(2,1)} %param.16) | copy-start | bytes 24580
  0.0 9.6 %copy-start.5 = (bf16[8,512]{1,0:T(8,128)(2,1)S(1)}, bf16[8,512]{1,0:T(8,128)(2,1)}, u32[]{:S(2)}) copy-start(bf16[8,512]{1,0:T(8,128)(2,1)} %param.12) | copy-start | bytes 24580
  0.0 10.3 %copy-start = (bf16[512,512]{1,0:T(8,128)(2,1)S(1)}, bf16[512,512]{1,0:T(8,128)(2,1)}, u32[]{:S(2)}) copy-start(bf16[512,512]{1,0:T(8,128)(2,1)} %factor_ref.1) | copy-start | bytes 1572868
  5.2 4.5 %collective-permute-start.2 = (f32[8,512]{1,0:T(8,128)S(1)}, f32[8,512]{1,0:T(8,128)S(1)}, u32[]{:S(2)}, u32[]{:S(2)}) collective-permute-start(f32[8,512]{1,0:T(8,128)S(1)} %reduce_sum.12), channel_id=1, source_target_pairs={{0,3},{1,0},{2,1},{3,2},{4,7},{5,4},{6,5},{7,6},{8,11},{9,8},{10,9... | collective-permute-start | bytes 49160 | tf_op jit(solution)/shard_map/ppermute | solution.py:172
  6.7 3.1 %collective-permute-start.1 = (f32[8,512]{1,0:T(8,128)S(1)}, f32[8,512]{1,0:T(8,128)S(1)}, u32[]{:S(2)}, u32[]{:S(2)}) collective-permute-start(f32[8,512]{1,0:T(8,128)S(1)} %reduce_sum.12), channel_id=1, source_target_pairs={{0,2},{1,3},{2,0},{3,1},{4,6},{5,7},{6,4},{7,5},{8,10},{9,11},{10,... | collective-permute-start | bytes 49160 | tf_op jit(solution)/shard_map/ppermute | solution.py:172
  8.1 2.2 collective-permute-start
  21.6 105.0 %copy-start.2 = (bf16[256,256]{1,0:T(8,128)(2,1)S(1)}, bf16[256,256]{1,0:T(8,128)(2,1)}, u32[]{:S(2)}) copy-start(bf16[256,256]{1,0:T(8,128)(2,1)} %second_ref.1) | copy-start | bytes 393220
  21.6 105.0 %copy-start.3 = (bf16[256,256]{1,0:T(8,128)(2,1)S(1)}, bf16[256,256]{1,0:T(8,128)(2,1)}, u32[]{:S(2)}) copy-start(bf16[256,256]{1,0:T(8,128)(2,1)} %inverse_ref.1) | copy-start | bytes 393220
  145.1 103.3 %copy-start.1 = (bf16[512,512]{1,0:T(8,128)(2,1)S(1)}, bf16[512,512]{1,0:T(8,128)(2,1)}, u32[]{:S(2)}) copy-start(bf16[512,512]{1,0:T(8,128)(2,1)} %refs_1_.1) | copy-start | bytes 1572868

commit v3 on v2

--- a/solution.py
+++ b/solution.py
@@ -1,3 +1,5 @@
+import functools
+
 import jax
 import jax.numpy as jnp
 from jax import lax
@@ -7,6 +9,7 @@
 
 LANES = 128
 TILE = 256
+CUTS = (((4,), (4,), "FR", True), ((1, 3), (1, 3), "FFRR", True))
 VMEM_LIMIT = 48 * 1024 * 1024
 
 
@@ -40,16 +43,17 @@
         out_ref[:, part * LANES : (part + 1) * LANES] = held[part].astype(jnp.bfloat16)
 
 
-def first_call(tokens, inv, gain, factor, tw):
-    rows, width = tokens.shape
+def first_call(tokens, inv, gain, factor, tw, start, tiles):
+    rows, _ = tokens.shape
+    width = tiles * TILE
     p_block, order = inv.shape
     return pl.pallas_call(
         first_kernel,
-        grid=(width // TILE,),
+        grid=(tiles,),
         in_specs=[
-            pl.BlockSpec((rows, TILE), lambda i: (0, i)),
+            pl.BlockSpec((rows, TILE), lambda i: (0, start + i)),
             pl.BlockSpec((p_block, order), lambda i: (0, 0)),
-            pl.BlockSpec((1, TILE), lambda i: (0, i)),
+            pl.BlockSpec((1, TILE), lambda i: (0, start + i)),
             pl.BlockSpec((order, order), lambda i: (0, 0)),
             pl.BlockSpec((order, p_block), lambda i: (0, 0)),
         ],
@@ -67,7 +71,8 @@
     )(tokens, inv, gain, factor, tw)
 
 
-def middle_kernel(v_ref, second_ref, gate_ref, inverse_ref, tw_ref, out_ref, tables, held, gates):
+def middle_kernel(v_ref, second_ref, gate_ref, inverse_ref, tw_ref, *rest):
+    out_ref, tables, held, gates = rest[-4:]
     groups, _, tile = v_ref.shape
     k_block, m_order, _ = tables.shape
     parts = held.shape[0]
@@ -102,22 +107,30 @@
         out_ref[:, part * LANES : (part + 1) * LANES] = held[part].astype(jnp.bfloat16)
 
 
-def middle_call(values, second, gate, inverse, tw):
-    groups, depth, width = values.shape
+def middle_call(values, second, gate, inverse, tw, so_far, at, to, start, tiles, width):
+    groups, depth, _ = values.shape
     m_order, k_block = tw.shape
     rows = groups * depth
+    in_specs = [
+        pl.BlockSpec((groups, depth, TILE), lambda i: (0, 0, at + i)),
+        pl.BlockSpec((m_order, m_order), lambda i: (0, 0)),
+        pl.BlockSpec((m_order, k_block, TILE), lambda i: (0, 0, start + i)),
+        pl.BlockSpec((m_order, m_order), lambda i: (0, 0)),
+        pl.BlockSpec((m_order, k_block), lambda i: (0, 0)),
+    ]
+    operands = [values, second, gate, inverse, tw]
+    aliases = {}
+    if so_far is not None:
+        in_specs.append(pl.BlockSpec(memory_space=pl.ANY))
+        aliases = {len(operands): 0}
+        operands.append(so_far)
     return pl.pallas_call(
         middle_kernel,
-        grid=(width // TILE,),
-        in_specs=[
-            pl.BlockSpec((groups, depth, TILE), lambda i: (0, 0, i)),
-            pl.BlockSpec((m_order, m_order), lambda i: (0, 0)),
-            pl.BlockSpec((m_order, k_block, TILE), lambda i: (0, 0, i)),
-            pl.BlockSpec((m_order, m_order), lambda i: (0, 0)),
-            pl.BlockSpec((m_order, k_block), lambda i: (0, 0)),
-        ],
-        out_specs=pl.BlockSpec((rows, TILE), lambda i: (0, i)),
+        grid=(tiles,),
+        in_specs=in_specs,
+        out_specs=pl.BlockSpec((rows, TILE), lambda i: (0, to + i)),
         out_shape=jax.ShapeDtypeStruct((rows, width), jnp.bfloat16),
+        input_output_aliases=aliases,
         scratch_shapes=[
             pltpu.VMEM((k_block, m_order, m_order), jnp.bfloat16),
             pltpu.VMEM((TILE // LANES, rows, LANES), jnp.float32),
@@ -125,13 +138,16 @@
         ],
         compiler_params=params(),
         cost_estimate=pl.CostEstimate(
-            flops=4 * rows * m_order * width, bytes_accessed=6 * rows * width, transcendentals=0
+            flops=4 * rows * m_order * tiles * TILE,
+            bytes_accessed=6 * rows * tiles * TILE,
+            transcendentals=0,
         ),
         name="middle_section",
-    )(values, second, gate, inverse, tw)
-
-
-def last_kernel(per, v_ref, factor_ref, out_ref):
+    )(*operands)
+
+
+def last_kernel(per, v_ref, factor_ref, *rest):
+    out_ref = rest[-1]
     groups, depth, width = v_ref.shape
     order = factor_ref.shape[0]
     for part in range(depth // per):
@@ -141,27 +157,39 @@
         ).astype(jnp.bfloat16)
 
 
-def last_call(values, factor):
+def last_call(values, factor, so_far, start, full_width):
     groups, depth, width = values.shape
     order = factor.shape[0]
     per = order // groups
-    steps = 2
     rows = groups * depth
+    whole = width == full_width
+    steps = 2 if whole else width // TILE
+    if whole:
+        in_block = pl.BlockSpec((groups, depth // steps, width), lambda i: (0, i, 0))
+        out_block = pl.BlockSpec((rows // steps, width), lambda i: (i, 0))
+    else:
+        in_block = pl.BlockSpec((groups, depth, TILE), lambda i: (0, 0, i))
+        out_block = pl.BlockSpec((rows, TILE), lambda i: (0, start + i))
+    in_specs = [in_block, pl.BlockSpec((order, order), lambda i: (0, 0))]
+    operands = [values, factor]
+    aliases = {}
+    if so_far is not None:
+        in_specs.append(pl.BlockSpec(memory_space=pl.ANY))
+        aliases = {len(operands): 0}
+        operands.append(so_far)
     return pl.pallas_call(
-        lambda *refs: last_kernel(per, *refs),
+        functools.partial(last_kernel, per),
         grid=(steps,),
-        in_specs=[
-            pl.BlockSpec((groups, depth // steps, width), lambda i: (0, i, 0)),
-            pl.BlockSpec((order, order), lambda i: (0, 0)),
-        ],
-        out_specs=pl.BlockSpec((rows // steps, width), lambda i: (i, 0)),
-        out_shape=jax.ShapeDtypeStruct((rows, width), jnp.bfloat16),
+        in_specs=in_specs,
+        out_specs=out_block,
+        out_shape=pltpu.HBM((rows, full_width), jnp.bfloat16),
+        input_output_aliases=aliases,
         compiler_params=params(),
         cost_estimate=pl.CostEstimate(
             flops=2 * rows * order * width, bytes_accessed=4 * rows * width, transcendentals=0
         ),
         name="last_section",
-    )(values, factor)
+    )(*operands)
 
 
 def chan_sum(part):
@@ -194,19 +222,58 @@
     square = chan_sum(jnp.sum(widened * widened, axis=2))
     inverse_rms = lax.rsqrt(square / (width_dev * lax.axis_size("chan")) + 1e-05)
 
-    sent = first_call(
-        tokens,
-        inverse_rms,
-        norm_gain.reshape(1, width_dev),
-        first_factor,
-        twiddle_in.T.astype(f32),
-    )
-    shape = (seq_count, rows_dev // seq_count, width_dev)
-    sent, tw_out = lax.optimization_barrier((sent.reshape(shape), twiddle_out.astype(f32)))
-    columns = lax.all_to_all(sent, "seq", split_axis=0, concat_axis=0, tiled=True)
-    back = middle_call(columns, second_factor, kernel_gate, second_inverse, tw_out)
-    returned = lax.all_to_all(back.reshape(shape), "seq", split_axis=0, concat_axis=0, tiled=True)
-    return last_call(returned, first_inverse)
+    gain = norm_gain.reshape(1, width_dev)
+    tw_in = twiddle_in.T.astype(f32)
+    inverse_rms, tw_out = lax.optimization_barrier((inverse_rms, twiddle_out.astype(f32)))
+
+    def exchange(values):
+        values = values.reshape(seq_count, rows_dev // seq_count, -1)
+        return lax.all_to_all(values, "seq", split_axis=0, concat_axis=0, tiled=True)
+
+    def cut(forward, backward, order, one_by_one, operands):
+        tokens, inv, gain, first_factor, tw_in, second, gate, inverse, tw_out, last = operands
+        arrived = []
+        returned = []
+        forward = list(forward)
+        backward = list(backward)
+        for step in order:
+            if step == "F":
+                tiles = forward.pop(0)
+                start = arrived[-1][1] if arrived else 0
+                values = exchange(first_call(tokens, inv, gain, first_factor, tw_in, start, tiles))
+            else:
+                tiles = backward.pop(0)
+                start = returned[-1][1] if returned else 0
+                values = None
+                for low, high, columns in arrived:
+                    first, end = max(low, start), min(high, start + tiles)
+                    if first < end:
+                        values = middle_call(
+                            columns, second, gate, inverse, tw_out, values,
+                            first - low, first - start, first, end - first, tiles * TILE,
+                        )
+                values = exchange(values)
+            if one_by_one:
+                values, inv, tw_out = lax.optimization_barrier((values, inv, tw_out))
+            (arrived if step == "F" else returned).append((start, start + tiles, values))
+        starts, _, values = zip(*returned)
+        if one_by_one:
+            values = lax.optimization_barrier(values)
+        out = None
+        for start, one in zip(starts, values):
+            out = last_call(one, last, out, start, width_dev)
+        return out
+
+    operands = (
+        tokens, inverse_rms, gain, first_factor, tw_in,
+        second_factor, kernel_gate, second_inverse, tw_out, first_inverse,
+    )
+    return lax.cond(
+        lax.axis_index("chan") % 2 == 0,
+        functools.partial(cut, *CUTS[0]),
+        functools.partial(cut, *CUTS[1]),
+        operands,
+    )
 
 
 def solution(mesh):

time: 259 us -> 242 us (0.934)
  blocking collectives: 208 us -> 188 us
  Pallas kernels: 38.7 us -> 42.6 us
    all_to_all x2 -> x4, blocking collectives: 208 us -> 188 us  [exchange(): lax.all_to_all(values, 'seq', split_axis=0, concat_axis=0, tiled=True)]
    pallas_call x3 -> x6, Pallas kernels: 38.7 us -> 42.6 us  [the longest x2 20.2 us: middle_call(): pl.pallas_call(middle_kernel, grid=(tiles,), in_specs=in_specs, out_specs...]
where the time goes in v3:
time: 242 us; the launch traced here: 241 us
  blocking collectives  188 us (78%)
  Pallas kernels  42.6 us (18%)
  other arithmetic  5.21 us (2%)
  starting transfers between devices  4.22 us (2%)
    all_to_all x4, blocking collectives, exchange(): lax.all_to_all(values, 'seq', split_axis=0, concat_axis=0, tiled=True)  188 us
    pallas_call x2, Pallas kernels, middle_call(): pl.pallas_call(middle_kernel, grid=(tiles,), in_specs=in_specs, out_specs...  20.2 us
    pallas_call x2, Pallas kernels, first_call(): pl.pallas_call(first_kernel, grid=(tiles,), in_specs=[pl.BlockSpec((rows,...  11.8 us
    pallas_call x2, Pallas kernels, last_call(): pl.pallas_call(functools.partial(last_kernel, per), grid=(steps,), in_spe...  10.7 us
    reduce_sum x1, other arithmetic, per_device(): square = chan_sum(jnp.sum(widened * widened, axis=2))  5.19 us
  transfers between devices with their start and end apart: 3, of which 1 were waited for; matrix products, arithmetic and copies ran while one was open for 0% of the time, Pallas kernels for 0%

profile of v3, /device:TPU:1, one launch (start us, length us, event | category | flops | bytes accessed | tf_op | source)
XLA Modules:
  0.0 241.4 jit_solution(16621348333981366172)
XLA Ops:
  0.0 0.0 copy-start.4
  0.0 0.0 copy-start.3
  0.0 5.2 %multiply_reduce_fusion = f32[4096]{0:T(1024)S(1)} fusion(bf16[4096,1024]{1,0:T(8,128)(2,1)} %param.11), kind=kLoop, calls=%fused_computation | loop fusion | flops 12578816 | bytes 8404992 | tf_op jit(solution)/shard_map/reduce_sum | solution.py:222
  5.3 1.5 collective-permute-start.2
  6.7 1.4 collective-permute-start.1
  8.1 1.3 collective-permute-start
  9.5 0.1 copy.25
  9.6 0.1 copy.26
  9.8 0.0 collective-permute-done.2
  9.8 0.0 collective-permute-done.1
  9.8 0.6 collective-permute-done
  10.4 231.0 %conditional.1 = (bf16[4096,1024]{1,0:T(8,128)(2,1)}) conditional(s32[]{:T(128)} %convert_element_type.16, (bf16[4096,1024]{1,0:T(8,128)(2,1)}, f32[8,512]{1,0:T(8,128)S(1)}, bf16[1024]{0:T(1024)(128)(2,1)S(1)}, bf16[512,512]{1,0:T(8,128)(2,1)S(1)}, f32[512,8]{1,0:T(8,128)S(1)}, /*index=5*/f32[256,16]{1,0:T(8,128)S(1)}, ...), branch_computations={%region_1.2_spmd, %region_2.3_spmd} | conditional | flops 12884901888 | bytes 125833256 | solution.py:271
  10.4 0.0 slice-start
  10.5 0.0 slice-start.1
  10.5 3.7 %first_section.3 = bf16[4096,256]{1,0:T(8,128)(2,1)S(1)} custom-call(bf16[4096,1024]{1,0:T(8,128)(2,1)} %get-tuple-element.48.x_ref, f32[8,512]{1,0:T(8,128)S(1)} %get-tuple-element.58.inv_ref, bf16[1,1024]{1,0:T(2,128)(2,1)S(1)} %reshape.24.gain_ref, bf16[512,512]{1,0:T(8,128)(2,1)S(1)} %get-tuple-element.100.factor_ref, f32[512,8]{1,0:T(8,128)S(1)} %get-tuple-element.52.tw_ref), custom_call_target="tpu_custom_call" | custom-call | flops 1073741824 | bytes 4194304 | tf_op jit(solution)/shard_map/cond/branch_0_fun/first_section/pallas_call | solution.py:50
  14.2 29.6 %all_to_all.24.v_ref = bf16[32,128,256]{2,1,0:T(8,128)(2,1)S(1)} all-to-all(bf16[32,128,256]{2,1,0:T(8,128)(2,1)S(1)} %bitcast.8), channel_id=1, replica_groups=mesh['seq'=32,'chan'=4] {'seq'}, dimensions={0} | all-to-all | bytes 4194304 | tf_op jit(solution)/shard_map/cond/branch_0_fun/all_to_all | solution.py:231
  43.8 8.1 %first_section.4 = bf16[4096,768]{1,0:T(8,128)(2,1)} custom-call(bf16[4096,1024]{1,0:T(8,128)(2,1)S(1)} %bitcast.10, f32[8,512]{1,0:T(8,128)S(1)} %get-tuple-element.58.inv_ref, bf16[1,1024]{1,0:T(2,128)(2,1)S(1)} %reshape.24.gain_ref, bf16[512,512]{1,0:T(8,128)(2,1)S(1)} %get-tuple-element.100.factor_ref, f32[512,8]{1,0:T(8,128)S(1)} %get-tuple-element.52.tw_ref), custom_call_target="tpu_custom_call" | custom-call | flops 3221225472 | bytes 12582912 | tf_op jit(solution)/shard_map/cond/branch_0_fun/first_section/pallas_call | solution.py:50
  51.9 69.5 %all_to_all.25.v_ref = bf16[32,128,768]{2,1,0:T(8,128)(2,1)} all-to-all(bf16[32,128,768]{2,1,0:T(8,128)(2,1)} %bitcast.13), channel_id=1, replica_groups=mesh['seq'=32,'chan'=4] {'seq'}, dimensions={0} | all-to-all | bytes 12582912 | tf_op jit(solution)/shard_map/cond/branch_0_fun/all_to_all | solution.py:231
  121.4 5.3 %middle_section.3 = bf16[4096,256]{1,0:T(8,128)(2,1)S(1)} custom-call(bf16[32,128,256]{2,1,0:T(8,128)(2,1)S(1)} %all_to_all.24.v_ref, bf16[256,256]{1,0:T(8,128)(2,1)S(1)} %get-tuple-element.102.second_ref, bf16[256,16,1024]{2,1,0:T(8,128)(2,1)} %get-tuple-element.104.gate_ref, bf16[256,256]{1,0:T(8,128)(2,1)S(1)} %get-tuple-element.106.inverse_ref, ...), custom_call_target="tpu_custom_call" | custom-call | flops 1073741824 | bytes 6291456 | tf_op jit(solution)/shard_map/cond/branch_0_fun/middle_section/pallas_call | solution.py:127
  126.7 24.4 %all_to_all.26.v_ref = bf16[32,128,256]{2,1,0:T(8,128)(2,1)S(1)} all-to-all(bf16[32,128,256]{2,1,0:T(8,128)(2,1)S(1)} %bitcast.7), channel_id=1, replica_groups=mesh['seq'=32,'chan'=4] {'seq'}, dimensions={0} | all-to-all | bytes 4194304 | tf_op jit(solution)/shard_map/cond/branch_0_fun/all_to_all | solution.py:231
  151.0 14.9 %middle_section.4 = bf16[4096,768]{1,0:T(8,128)(2,1)} custom-call(bf16[32,128,768]{2,1,0:T(8,128)(2,1)} %all_to_all.25.v_ref, bf16[256,256]{1,0:T(8,128)(2,1)S(1)} %get-tuple-element.102.second_ref, bf16[256,16,1024]{2,1,0:T(8,128)(2,1)} %get-tuple-element.104.gate_ref, bf16[256,256]{1,0:T(8,128)(2,1)S(1)} %get-tuple-element.106.inverse_ref, ...), custom_call_target="tpu_custom_call" | custom-call | flops 3221225472 | bytes 18874368 | tf_op jit(solution)/shard_map/cond/branch_0_fun/middle_section/pallas_call | solution.py:127
  165.9 64.8 %all_to_all.27.v_ref = bf16[32,128,768]{2,1,0:T(8,128)(2,1)} all-to-all(bf16[32,128,768]{2,1,0:T(8,128)(2,1)} %bitcast.14), channel_id=1, replica_groups=mesh['seq'=32,'chan'=4] {'seq'}, dimensions={0} | all-to-all | bytes 12582912 | tf_op jit(solution)/shard_map/cond/branch_0_fun/all_to_all | solution.py:231
  230.7 2.6 %last_section.3.rest_0_ = bf16[4096,1024]{1,0:T(8,128)(2,1)} custom-call(bf16[32,128,256]{2,1,0:T(8,128)(2,1)S(1)} %all_to_all.26.v_ref, bf16[512,512]{1,0:T(8,128)(2,1)S(1)} %get-tuple-element.108.factor_ref), custom_call_target="tpu_custom_call" | custom-call | flops 1073741824 | bytes 4194304 | tf_op jit(solution)/shard_map/cond/branch_0_fun/last_section/pallas_call | solution.py:180
  233.3 8.1 %last_section.4 = bf16[4096,1024]{1,0:T(8,128)(2,1)} custom-call(bf16[32,128,768]{2,1,0:T(8,128)(2,1)} %all_to_all.27.v_ref, bf16[512,512]{1,0:T(8,128)(2,1)S(1)} %get-tuple-element.108.factor_ref, bf16[4096,1024]{1,0:T(8,128)(2,1)} %last_section.3.rest_0_), custom_call_target="tpu_custom_call", output_to_operand_aliasing={{}: (2, {})} | custom-call | flops 3221225472 | bytes 12582912 | tf_op jit(solution)/shard_map/cond/branch_0_fun/last_section/pallas_call | solution.py:180
  (19 shorter events, 0.1 us)
Async XLA Ops:
  0.0 9.5 %copy-start.5 = (bf16[256,16]{0,1:T(8,128)(2,1)S(1)}, bf16[256,16]{0,1:T(8,128)(2,1)}, u32[]{:S(2)}) copy-start(bf16[256,16]{0,1:T(8,128)(2,1)} %param.18) | copy-start | bytes 24580
  0.0 9.6 %copy-start.6 = (bf16[8,512]{1,0:T(8,128)(2,1)S(1)}, bf16[8,512]{1,0:T(8,128)(2,1)}, u32[]{:S(2)}) copy-start(bf16[8,512]{1,0:T(8,128)(2,1)} %param.14) | copy-start | bytes 24580
  0.0 10.4 %copy-start.2 = (bf16[512,512]{1,0:T(8,128)(2,1)S(1)}, bf16[512,512]{1,0:T(8,128)(2,1)}, u32[]{:S(2)}) copy-start(bf16[512,512]{1,0:T(8,128)(2,1)} %param.19) | copy-start | bytes 1572868
  0.0 10.4 %copy-start.4 = (bf16[256,256]{1,0:T(8,128)(2,1)S(1)}, bf16[256,256]{1,0:T(8,128)(2,1)}, u32[]{:S(2)}) copy-start(bf16[256,256]{1,0:T(8,128)(2,1)} %param.17) | copy-start | bytes 393220
  0.0 10.4 %copy-start.3 = (bf16[256,256]{1,0:T(8,128)(2,1)S(1)}, bf16[256,256]{1,0:T(8,128)(2,1)}, u32[]{:S(2)}) copy-start(bf16[256,256]{1,0:T(8,128)(2,1)} %param.15) | copy-start | bytes 393220
  0.0 10.4 %copy-start.1 = (bf16[512,512]{1,0:T(8,128)(2,1)S(1)}, bf16[512,512]{1,0:T(8,128)(2,1)}, u32[]{:S(2)}) copy-start(bf16[512,512]{1,0:T(8,128)(2,1)} %param.13) | copy-start | bytes 1572868
  0.0 10.4 %copy-start.7 = (bf16[1024]{0:T(1024)(128)(2,1)S(1)}, bf16[1024]{0:T(1024)(128)(2,1)}, u32[]{:S(2)}) copy-start(bf16[1024]{0:T(1024)(128)(2,1)} %param.12) | copy-start | bytes 6148
  5.3 4.5 %collective-permute-start.2 = (f32[8,512]{1,0:T(8,128)S(1)}, f32[8,512]{1,0:T(8,128)S(1)}, u32[]{:S(2)}, u32[]{:S(2)}) collective-permute-start(f32[8,512]{1,0:T(8,128)S(1)} %reduce_sum.12), channel_id=1, source_target_pairs={{0,3},{1,0},{2,1},{3,2},{4,7},{5,4},{6,5},{7,6},{8,11},{9,8},{10,9... | collective-permute-start | bytes 49160 | tf_op jit(solution)/shard_map/ppermute | solution.py:200
  6.7 3.0 %collective-permute-start.1 = (f32[8,512]{1,0:T(8,128)S(1)}, f32[8,512]{1,0:T(8,128)S(1)}, u32[]{:S(2)}, u32[]{:S(2)}) collective-permute-start(f32[8,512]{1,0:T(8,128)S(1)} %reduce_sum.12), channel_id=1, source_target_pairs={{0,2},{1,3},{2,0},{3,1},{4,6},{5,7},{6,4},{7,5},{8,10},{9,11},{10,... | collective-permute-start | bytes 49160 | tf_op jit(solution)/shard_map/ppermute | solution.py:200
  8.1 2.2 collective-permute-start
  10.4 33.4 %slice-start = ((s8[8388608]{0:T(1024)(128)(4,1)}), s8[4194304]{0:T(1024)(128)(4,1)S(1)}, s32[]{:S(2)}) async-start(s8[8388608]{0:T(1024)(128)(4,1)} %bitcast.9), calls=%async_computation.6 | async-start | bytes 8388608 | tf_op jit(solution)/shard_map/cond
  10.5 33.4 %slice-start.1 = ((s8[8388608]{0:T(1024)(128)(4,1)}), s8[4194304]{0:T(1024)(128)(4,1)S(1)}, s32[]{:S(2)}) async-start(s8[8388608]{0:T(1024)(128)(4,1)} %bitcast.9), calls=%async_computation.7 | async-start | bytes 8388608 | tf_op jit(solution)/shard_map/cond

commit v4 on v3

--- a/solution.py
+++ b/solution.py
@@ -9,13 +9,13 @@
 
 LANES = 128
 TILE = 256
-CUTS = (((4,), (4,), "FR", True), ((1, 3), (1, 3), "FFRR", True))
+CUTS = (((4,), (4,), "FR", True), ((1, 1, 2), (4,), "FFFR", True))
 VMEM_LIMIT = 48 * 1024 * 1024
 
 
-def params():
+def params(axes=1):
     return pltpu.CompilerParams(
-        dimension_semantics=("arbitrary",), vmem_limit_bytes=VMEM_LIMIT
+        dimension_semantics=("arbitrary",) * axes, vmem_limit_bytes=VMEM_LIMIT
     )
 
 
@@ -163,14 +163,10 @@
     per = order // groups
     rows = groups * depth
     whole = width == full_width
-    steps = 2 if whole else width // TILE
-    if whole:
-        in_block = pl.BlockSpec((groups, depth // steps, width), lambda i: (0, i, 0))
-        out_block = pl.BlockSpec((rows // steps, width), lambda i: (i, 0))
-    else:
-        in_block = pl.BlockSpec((groups, depth, TILE), lambda i: (0, 0, i))
-        out_block = pl.BlockSpec((rows, TILE), lambda i: (0, start + i))
-    in_specs = [in_block, pl.BlockSpec((order, order), lambda i: (0, 0))]
+    tile = width if whole else TILE
+    in_block = pl.BlockSpec((groups, depth // 2, tile), lambda i, j: (0, j, i))
+    out_block = pl.BlockSpec((rows // 2, tile), lambda i, j: (j, start + i))
+    in_specs = [in_block, pl.BlockSpec((order, order), lambda i, j: (0, 0))]
     operands = [values, factor]
     aliases = {}
     if so_far is not None:
@@ -179,12 +175,12 @@
         operands.append(so_far)
     return pl.pallas_call(
         functools.partial(last_kernel, per),
-        grid=(steps,),
+        grid=(width // tile, 2),
         in_specs=in_specs,
         out_specs=out_block,
         out_shape=pltpu.HBM((rows, full_width), jnp.bfloat16),
         input_output_aliases=aliases,
-        compiler_params=params(),
+        compiler_params=params(2),
         cost_estimate=pl.CostEstimate(
             flops=2 * rows * order * width, bytes_accessed=4 * rows * width, transcendentals=0
         ),

time: 242 us -> 234 us (0.967)
  blocking collectives: 188 us -> 177 us
    all_to_all x4, blocking collectives: 188 us -> 177 us  [exchange(): lax.all_to_all(values, 'seq', split_axis=0, concat_axis=0, tiled=True)]
    pallas_call x2 -> x3, Pallas kernels: 20.2 us -> 23.9 us  [middle_call(): pl.pallas_call(middle_kernel, grid=(tiles,), in_specs=in_specs, out_specs...]
    pallas_call x2 -> x1, Pallas kernels: 10.7 us -> 8.92 us  [last_call(): pl.pallas_call(functools.partial(last_kernel, per), grid=(width // tile,...]
    pallas_call x2 -> x3, Pallas kernels: 11.8 us -> 11.9 us  [first_call(): pl.pallas_call(first_kernel, grid=(tiles,), in_specs=[pl.BlockSpec((rows,...]
where the time goes in v4:
time: 234 us; the launch traced here: 232 us
  blocking collectives  177 us (76%)
  Pallas kernels  44.8 us (19%)
  other arithmetic  5.21 us (2%)
  starting transfers between devices  4.22 us (2%)
    all_to_all x4, blocking collectives, exchange(): lax.all_to_all(values, 'seq', split_axis=0, concat_axis=0, tiled=True)  177 us
    pallas_call x3, Pallas kernels, middle_call(): pl.pallas_call(middle_kernel, grid=(tiles,), in_specs=in_specs, out_specs...  23.9 us
    pallas_call x3, Pallas kernels, first_call(): pl.pallas_call(first_kernel, grid=(tiles,), in_specs=[pl.BlockSpec((rows,...  11.9 us
    pallas_call x1, Pallas kernels, last_call(): pl.pallas_call(functools.partial(last_kernel, per), grid=(width // tile,...  8.92 us
    reduce_sum x1, other arithmetic, per_device(): square = chan_sum(jnp.sum(widened * widened, axis=2))  5.19 us
  transfers between devices with their start and end apart: 3, of which 1 were waited for; matrix products, arithmetic and copies ran while one was open for 0% of the time, Pallas kernels for 0%

profile of v4, /device:TPU:1, one launch (start us, length us, event | category | flops | bytes accessed | tf_op | source)
XLA Modules:
  0.0 231.9 jit_solution(2767318824405559327)
XLA Ops:
  0.0 5.2 %multiply_reduce_fusion = f32[4096]{0:T(1024)S(1)} fusion(bf16[4096,1024]{1,0:T(8,128)(2,1)} %param.11), kind=kLoop, calls=%fused_computation | loop fusion | flops 12578816 | bytes 8404992 | tf_op jit(solution)/shard_map/reduce_sum | solution.py:218
  5.3 1.5 collective-permute-start.2
  6.7 1.4 collective-permute-start.1
  8.1 1.3 collective-permute-start
  9.5 0.1 copy.26
  9.6 0.1 copy.27
  9.8 0.0 collective-permute-done.2
  9.8 0.0 collective-permute-done.1
  9.8 0.6 collective-permute-done
  10.4 0.0 copy-done.4
  10.4 221.5 %conditional.1 = (bf16[4096,1024]{1,0:T(8,128)(2,1)}) conditional(s32[]{:T(128)} %convert_element_type.16, (bf16[4096,1024]{1,0:T(8,128)(2,1)}, f32[8,512]{1,0:T(8,128)S(1)}, bf16[1024]{0:T(1024)(128)(2,1)S(1)}, bf16[512,512]{1,0:T(8,128)(2,1)S(1)}, f32[512,8]{1,0:T(8,128)S(1)}, /*index=5*/f32[256,16]{1,0:T(8,128)S(1)}, ...), branch_computations={%region_1.2_spmd, %region_2.3_spmd} | conditional | flops 12884901888 | bytes 125833256 | solution.py:267
  10.4 0.0 slice-start
  10.5 0.0 slice-start.1
  10.5 3.7 %first_section.4 = bf16[4096,256]{1,0:T(8,128)(2,1)S(1)} custom-call(bf16[4096,1024]{1,0:T(8,128)(2,1)} %get-tuple-element.48.x_ref, f32[8,512]{1,0:T(8,128)S(1)} %get-tuple-element.56.inv_ref, bf16[1,1024]{1,0:T(2,128)(2,1)S(1)} %reshape.24.gain_ref, bf16[512,512]{1,0:T(8,128)(2,1)S(1)} %get-tuple-element.99.factor_ref, f32[512,8]{1,0:T(8,128)S(1)} %get-tuple-element.52.tw_ref), custom_call_target="tpu_custom_call" | custom-call | flops 1073741824 | bytes 4194304 | tf_op jit(solution)/shard_map/cond/branch_0_fun/first_section/pallas_call | solution.py:50
  14.2 29.6 %all_to_all.24.v_ref = bf16[32,128,256]{2,1,0:T(8,128)(2,1)S(1)} all-to-all(bf16[32,128,256]{2,1,0:T(8,128)(2,1)S(1)} %bitcast.8), channel_id=1, replica_groups=mesh['seq'=32,'chan'=4] {'seq'}, dimensions={0} | all-to-all | bytes 4194304 | tf_op jit(solution)/shard_map/cond/branch_0_fun/all_to_all | solution.py:227
  43.8 2.0 first_section.5
  45.9 37.5 %all_to_all.25.v_ref = bf16[32,128,256]{2,1,0:T(8,128)(2,1)S(1)} all-to-all(bf16[32,128,256]{2,1,0:T(8,128)(2,1)S(1)} %bitcast.9), channel_id=1, replica_groups=mesh['seq'=32,'chan'=4] {'seq'}, dimensions={0} | all-to-all | bytes 4194304 | tf_op jit(solution)/shard_map/cond/branch_0_fun/all_to_all | solution.py:227
  83.4 6.1 %first_section.6 = bf16[4096,512]{1,0:T(8,128)(2,1)S(1)} custom-call(bf16[4096,1024]{1,0:T(8,128)(2,1)} %get-tuple-element.48.x_ref, f32[8,512]{1,0:T(8,128)S(1)} %get-tuple-element.56.inv_ref, bf16[1,1024]{1,0:T(2,128)(2,1)S(1)} %reshape.24.gain_ref, bf16[512,512]{1,0:T(8,128)(2,1)S(1)} %get-tuple-element.99.factor_ref, f32[512,8]{1,0:T(8,128)S(1)} %get-tuple-element.52.tw_ref), custom_call_target="tpu_custom_call" | custom-call | flops 2147483648 | bytes 8388608 | tf_op jit(solution)/shard_map/cond/branch_0_fun/first_section/pallas_call | solution.py:50
  89.5 38.0 %all_to_all.26.v_ref = bf16[32,128,512]{2,1,0:T(8,128)(2,1)S(1)} all-to-all(bf16[32,128,512]{2,1,0:T(8,128)(2,1)S(1)} %bitcast.7), channel_id=1, replica_groups=mesh['seq'=32,'chan'=4] {'seq'}, dimensions={0} | all-to-all | bytes 8388608 | tf_op jit(solution)/shard_map/cond/branch_0_fun/all_to_all | solution.py:227
  127.5 6.6 %middle_section.4.rest_0_ = bf16[4096,1024]{1,0:T(8,128)(2,1)} custom-call(bf16[32,128,256]{2,1,0:T(8,128)(2,1)S(1)} %all_to_all.24.v_ref, bf16[256,256]{1,0:T(8,128)(2,1)S(1)} %get-tuple-element.101.second_ref, bf16[256,16,1024]{2,1,0:T(8,128)(2,1)} %get-tuple-element.103.gate_ref, bf16[256,256]{1,0:T(8,128)(2,1)S(1)} %get-tuple-element.105.inverse_ref, ...), custom_call_target="tpu_custom_call" | custom-call | flops 1073741824 | bytes 6291456 | tf_op jit(solution)/shard_map/cond/branch_0_fun/middle_section/pallas_call | solution.py:127
  134.1 6.6 %middle_section.5.rest_0_ = bf16[4096,1024]{1,0:T(8,128)(2,1)} custom-call(bf16[32,128,256]{2,1,0:T(8,128)(2,1)S(1)} %all_to_all.25.v_ref, bf16[256,256]{1,0:T(8,128)(2,1)S(1)} %get-tuple-element.101.second_ref, bf16[256,16,1024]{2,1,0:T(8,128)(2,1)} %get-tuple-element.103.gate_ref, ...), custom_call_target="tpu_custom_call", output_to_operand_aliasing={{}: (5, {})} | custom-call | flops 1073741824 | bytes 6291456 | tf_op jit(solution)/shard_map/cond/branch_0_fun/middle_section/pallas_call | solution.py:127
  140.7 10.8 %middle_section.6 = bf16[4096,1024]{1,0:T(8,128)(2,1)} custom-call(bf16[32,128,512]{2,1,0:T(8,128)(2,1)S(1)} %all_to_all.26.v_ref, bf16[256,256]{1,0:T(8,128)(2,1)S(1)} %get-tuple-element.101.second_ref, bf16[256,16,1024]{2,1,0:T(8,128)(2,1)} %get-tuple-element.103.gate_ref, ...), custom_call_target="tpu_custom_call", output_to_operand_aliasing={{}: (5, {})} | custom-call | flops 2147483648 | bytes 12582912 | tf_op jit(solution)/shard_map/cond/branch_0_fun/middle_section/pallas_call | solution.py:127
  151.4 71.5 %all_to_all.27.v_ref = bf16[32,128,1024]{2,1,0:T(8,128)(2,1)} all-to-all(bf16[32,128,1024]{2,1,0:T(8,128)(2,1)} %bitcast.12), channel_id=1, replica_groups=mesh['seq'=32,'chan'=4] {'seq'}, dimensions={0} | all-to-all | bytes 16777216 | tf_op jit(solution)/shard_map/cond/branch_0_fun/all_to_all | solution.py:227
  223.0 8.9 %last_section.2 = bf16[4096,1024]{1,0:T(8,128)(2,1)} custom-call(bf16[32,128,1024]{2,1,0:T(8,128)(2,1)} %all_to_all.27.v_ref, bf16[512,512]{1,0:T(8,128)(2,1)S(1)} %get-tuple-element.107.factor_ref), custom_call_target="tpu_custom_call" | custom-call | flops 4294967296 | bytes 16777216 | tf_op jit(solution)/shard_map/cond/branch_0_fun/last_section/pallas_call | solution.py:176
  (20 shorter events, 0.1 us)
Async XLA Ops:
  0.0 9.5 %copy-start.5 = (bf16[256,16]{0,1:T(8,128)(2,1)S(1)}, bf16[256,16]{0,1:T(8,128)(2,1)}, u32[]{:S(2)}) copy-start(bf16[256,16]{0,1:T(8,128)(2,1)} %param.18) | copy-start | bytes 24580
  0.0 9.6 %copy-start.6 = (bf16[8,512]{1,0:T(8,128)(2,1)S(1)}, bf16[8,512]{1,0:T(8,128)(2,1)}, u32[]{:S(2)}) copy-start(bf16[8,512]{1,0:T(8,128)(2,1)} %param.14) | copy-start | bytes 24580
  0.0 10.4 %copy-start.4 = (bf16[512,512]{1,0:T(8,128)(2,1)S(1)}, bf16[512,512]{1,0:T(8,128)(2,1)}, u32[]{:S(2)}) copy-start(bf16[512,512]{1,0:T(8,128)(2,1)} %param.19) | copy-start | bytes 1572868
  0.0 10.4 %copy-start.3 = (bf16[256,256]{1,0:T(8,128)(2,1)S(1)}, bf16[256,256]{1,0:T(8,128)(2,1)}, u32[]{:S(2)}) copy-start(bf16[256,256]{1,0:T(8,128)(2,1)} %param.17) | copy-start | bytes 393220
  0.0 10.4 %copy-start.2 = (bf16[256,256]{1,0:T(8,128)(2,1)S(1)}, bf16[256,256]{1,0:T(8,128)(2,1)}, u32[]{:S(2)}) copy-start(bf16[256,256]{1,0:T(8,128)(2,1)} %param.15) | copy-start | bytes 393220
  0.0 10.4 %copy-start.1 = (bf16[512,512]{1,0:T(8,128)(2,1)S(1)}, bf16[512,512]{1,0:T(8,128)(2,1)}, u32[]{:S(2)}) copy-start(bf16[512,512]{1,0:T(8,128)(2,1)} %param.13) | copy-start | bytes 1572868
  0.0 10.4 %copy-start.7 = (bf16[1024]{0:T(1024)(128)(2,1)S(1)}, bf16[1024]{0:T(1024)(128)(2,1)}, u32[]{:S(2)}) copy-start(bf16[1024]{0:T(1024)(128)(2,1)} %param.12) | copy-start | bytes 6148
  5.3 4.5 %collective-permute-start.2 = (f32[8,512]{1,0:T(8,128)S(1)}, f32[8,512]{1,0:T(8,128)S(1)}, u32[]{:S(2)}, u32[]{:S(2)}) collective-permute-start(f32[8,512]{1,0:T(8,128)S(1)} %reduce_sum.12), channel_id=1, source_target_pairs={{0,3},{1,0},{2,1},{3,2},{4,7},{5,4},{6,5},{7,6},{8,11},{9,8},{10,9... | collective-permute-start | bytes 49160 | tf_op jit(solution)/shard_map/ppermute | solution.py:196
  6.7 3.0 %collective-permute-start.1 = (f32[8,512]{1,0:T(8,128)S(1)}, f32[8,512]{1,0:T(8,128)S(1)}, u32[]{:S(2)}, u32[]{:S(2)}) collective-permute-start(f32[8,512]{1,0:T(8,128)S(1)} %reduce_sum.12), channel_id=1, source_target_pairs={{0,2},{1,3},{2,0},{3,1},{4,6},{5,7},{6,4},{7,5},{8,10},{9,11},{10,... | collective-permute-start | bytes 49160 | tf_op jit(solution)/shard_map/ppermute | solution.py:196
  8.1 2.2 collective-permute-start
  10.4 33.4 %slice-start = ((s8[8388608]{0:T(1024)(128)(4,1)}), s8[4194304]{0:T(1024)(128)(4,1)S(1)}, s32[]{:S(2)}) async-start(s8[8388608]{0:T(1024)(128)(4,1)} %bitcast.10), calls=%async_computation.6 | async-start | bytes 8388608 | tf_op jit(solution)/shard_map/cond
  10.5 33.4 %slice-start.1 = ((s8[8388608]{0:T(1024)(128)(4,1)}), s8[4194304]{0:T(1024)(128)(4,1)S(1)}, s32[]{:S(2)}) async-start(s8[8388608]{0:T(1024)(128)(4,1)} %bitcast.10), calls=%async_computation.7 | async-start | bytes 8388608 | tf_op jit(solution)/shard_map/cond

commit v5 on v4

--- a/solution.py
+++ b/solution.py
@@ -71,8 +71,20 @@
     )(tokens, inv, gain, factor, tw)
 
 
-def middle_kernel(v_ref, second_ref, gate_ref, inverse_ref, tw_ref, *rest):
-    out_ref, tables, held, gates = rest[-4:]
+def middle_kernel(spans, *refs):
+    sources = refs[: len(spans)]
+    others = refs[len(spans) :]
+    if len(spans) == 1:
+        middle_tile(sources[0], *others)
+        return
+    step = pl.program_id(0)
+    for (low, high), source in zip(spans, sources):
+        pl.when(jnp.logical_and(step >= low, step < high))(
+            functools.partial(middle_tile, source, *others)
+        )
+
+
+def middle_tile(v_ref, second_ref, gate_ref, inverse_ref, tw_ref, out_ref, tables, held, gates):
     groups, _, tile = v_ref.shape
     k_block, m_order, _ = tables.shape
     parts = held.shape[0]
@@ -107,30 +119,32 @@
         out_ref[:, part * LANES : (part + 1) * LANES] = held[part].astype(jnp.bfloat16)
 
 
-def middle_call(values, second, gate, inverse, tw, so_far, at, to, start, tiles, width):
-    groups, depth, _ = values.shape
+def middle_call(parts, second, gate, inverse, tw, start, tiles):
+    groups, depth, _ = parts[0][3].shape
     m_order, k_block = tw.shape
     rows = groups * depth
-    in_specs = [
-        pl.BlockSpec((groups, depth, TILE), lambda i: (0, 0, at + i)),
+    in_specs = []
+    for low, count, at, _ in parts:
+        in_specs.append(
+            pl.BlockSpec(
+                (groups, depth, TILE),
+                lambda i, low=low, count=count, at=at: (0, 0, at + jnp.clip(i - low, 0, count - 1)),
+            )
+        )
+    in_specs += [
         pl.BlockSpec((m_order, m_order), lambda i: (0, 0)),
         pl.BlockSpec((m_order, k_block, TILE), lambda i: (0, 0, start + i)),
         pl.BlockSpec((m_order, m_order), lambda i: (0, 0)),
         pl.BlockSpec((m_order, k_block), lambda i: (0, 0)),
     ]
-    operands = [values, second, gate, inverse, tw]
-    aliases = {}
-    if so_far is not None:
-        in_specs.append(pl.BlockSpec(memory_space=pl.ANY))
-        aliases = {len(operands): 0}
-        operands.append(so_far)
+    operands = [part[3] for part in parts] + [second, gate, inverse, tw]
+    spans = tuple((low, low + count) for low, count, _, _ in parts)
     return pl.pallas_call(
-        middle_kernel,
+        functools.partial(middle_kernel, spans),
         grid=(tiles,),
         in_specs=in_specs,
-        out_specs=pl.BlockSpec((rows, TILE), lambda i: (0, to + i)),
-        out_shape=jax.ShapeDtypeStruct((rows, width), jnp.bfloat16),
-        input_output_aliases=aliases,
+        out_specs=pl.BlockSpec((rows, TILE), lambda i: (0, i)),
+        out_shape=jax.ShapeDtypeStruct((rows, tiles * TILE), jnp.bfloat16),
         scratch_shapes=[
             pltpu.VMEM((k_block, m_order, m_order), jnp.bfloat16),
             pltpu.VMEM((TILE // LANES, rows, LANES), jnp.float32),
@@ -240,14 +254,12 @@
             else:
                 tiles = backward.pop(0)
                 start = returned[-1][1] if returned else 0
-                values = None
+                parts = []
                 for low, high, columns in arrived:
                     first, end = max(low, start), min(high, start + tiles)
                     if first < end:
-                        values = middle_call(
-                            columns, second, gate, inverse, tw_out, values,
-                            first - low, first - start, first, end - first, tiles * TILE,
-                        )
+                        parts.append((first - start, end - first, first - low, columns))
+                values = middle_call(parts, second, gate, inverse, tw_out, start, tiles)
                 values = exchange(values)
             if one_by_one:
                 values, inv, tw_out = lax.optimization_barrier((values, inv, tw_out))

time: 234 us -> 232 us (level)
  Pallas kernels: 44.8 us -> 39.5 us
  blocking collectives: 177 us -> 182 us
    all_to_all x4, blocking collectives: 177 us -> 182 us  [exchange(): lax.all_to_all(values, 'seq', split_axis=0, concat_axis=0, tiled=True)]
    pallas_call x3 -> x1, Pallas kernels: 23.9 us -> 18.7 us  [middle_call(): pl.pallas_call(functools.partial(middle_kernel, spans), grid=(tiles,), in...]
where the time goes in v5:
time: 232 us
  blocking collectives  182 us (78%)
  Pallas kernels  39.5 us (17%)
  other arithmetic  5.21 us (2%)
  starting transfers between devices  4.22 us (2%)
    all_to_all x4, blocking collectives, exchange(): lax.all_to_all(values, 'seq', split_axis=0, concat_axis=0, tiled=True)  182 us
    pallas_call x1, Pallas kernels, middle_call(): pl.pallas_call(functools.partial(middle_kernel, spans), grid=(tiles,), in...  18.7 us
    pallas_call x3, Pallas kernels, first_call(): pl.pallas_call(first_kernel, grid=(tiles,), in_specs=[pl.BlockSpec((rows,...  11.9 us
    pallas_call x1, Pallas kernels, last_call(): pl.pallas_call(functools.partial(last_kernel, per), grid=(width // tile,...  8.92 us
    reduce_sum x1, other arithmetic, per_device(): square = chan_sum(jnp.sum(widened * widened, axis=2))  5.19 us
  transfers between devices with their start and end apart: 3, of which 1 were waited for; matrix products, arithmetic and copies ran while one was open for 0% of the time, Pallas kernels for 0%

profile of v5, /device:TPU:1, one launch (start us, length us, event | category | flops | bytes accessed | tf_op | source)
XLA Modules:
  0.0 231.9 jit_solution(6122340359351982783)
XLA Ops:
  0.0 0.0 copy-start.4
  0.0 0.0 copy-start.3
  0.0 0.0 copy-start.1
  0.0 5.2 %multiply_reduce_fusion = f32[4096]{0:T(1024)S(1)} fusion(bf16[4096,1024]{1,0:T(8,128)(2,1)} %param.11), kind=kLoop, calls=%fused_computation | loop fusion | flops 12578816 | bytes 8404992 | tf_op jit(solution)/shard_map/reduce_sum | solution.py:232
  5.3 1.5 collective-permute-start.2
  6.7 1.4 collective-permute-start.1
  8.1 1.3 collective-permute-start
  9.5 0.1 copy.24
  9.6 0.1 copy.25
  9.8 0.0 collective-permute-done.2
  9.8 0.0 collective-permute-done.1
  9.8 0.6 collective-permute-done
  10.4 221.5 %conditional.1 = (bf16[4096,1024]{1,0:T(8,128)(2,1)}) conditional(s32[]{:T(128)} %convert_element_type.16, (bf16[4096,1024]{1,0:T(8,128)(2,1)}, f32[8,512]{1,0:T(8,128)S(1)}, bf16[1024]{0:T(1024)(128)(2,1)S(1)}, bf16[512,512]{1,0:T(8,128)(2,1)S(1)}, f32[512,8]{1,0:T(8,128)S(1)}, /*index=5*/f32[256,16]{1,0:T(8,128)S(1)}, ...), branch_computations={%region_1.2_spmd, %region_2.3_spmd} | conditional | flops 12884901888 | bytes 125833256 | solution.py:279
  10.4 0.0 slice-start
  10.5 0.0 slice-start.1
  10.5 3.7 %first_section.4 = bf16[4096,256]{1,0:T(8,128)(2,1)S(1)} custom-call(bf16[4096,1024]{1,0:T(8,128)(2,1)} %get-tuple-element.48.x_ref, f32[8,512]{1,0:T(8,128)S(1)} %get-tuple-element.58.inv_ref, bf16[1,1024]{1,0:T(2,128)(2,1)S(1)} %reshape.24.gain_ref, bf16[512,512]{1,0:T(8,128)(2,1)S(1)} %get-tuple-element.99.factor_ref, f32[512,8]{1,0:T(8,128)S(1)} %get-tuple-element.52.tw_ref), custom_call_target="tpu_custom_call" | custom-call | flops 1073741824 | bytes 4194304 | tf_op jit(solution)/shard_map/cond/branch_0_fun/first_section/pallas_call | solution.py:50
  14.2 29.6 %all_to_all.24.refs_0_ = bf16[32,128,256]{2,1,0:T(8,128)(2,1)S(1)} all-to-all(bf16[32,128,256]{2,1,0:T(8,128)(2,1)S(1)} %bitcast.8), channel_id=1, replica_groups=mesh['seq'=32,'chan'=4] {'seq'}, dimensions={0} | all-to-all | bytes 4194304 | tf_op jit(solution)/shard_map/cond/branch_0_fun/all_to_all | solution.py:241
  43.8 2.0 first_section.5
  45.9 37.5 %all_to_all.25.refs_1_ = bf16[32,128,256]{2,1,0:T(8,128)(2,1)S(1)} all-to-all(bf16[32,128,256]{2,1,0:T(8,128)(2,1)S(1)} %bitcast.9), channel_id=1, replica_groups=mesh['seq'=32,'chan'=4] {'seq'}, dimensions={0} | all-to-all | bytes 4194304 | tf_op jit(solution)/shard_map/cond/branch_0_fun/all_to_all | solution.py:241
  83.4 6.1 %first_section.6 = bf16[4096,512]{1,0:T(8,128)(2,1)S(1)} custom-call(bf16[4096,1024]{1,0:T(8,128)(2,1)} %get-tuple-element.48.x_ref, f32[8,512]{1,0:T(8,128)S(1)} %get-tuple-element.58.inv_ref, bf16[1,1024]{1,0:T(2,128)(2,1)S(1)} %reshape.24.gain_ref, bf16[512,512]{1,0:T(8,128)(2,1)S(1)} %get-tuple-element.99.factor_ref, f32[512,8]{1,0:T(8,128)S(1)} %get-tuple-element.52.tw_ref), custom_call_target="tpu_custom_call" | custom-call | flops 2147483648 | bytes 8388608 | tf_op jit(solution)/shard_map/cond/branch_0_fun/first_section/pallas_call | solution.py:50
  89.5 38.1 %all_to_all.26.refs_2_ = bf16[32,128,512]{2,1,0:T(8,128)(2,1)} all-to-all(bf16[32,128,512]{2,1,0:T(8,128)(2,1)S(1)} %bitcast.7), channel_id=1, replica_groups=mesh['seq'=32,'chan'=4] {'seq'}, dimensions={0} | all-to-all | bytes 8388608 | tf_op jit(solution)/shard_map/cond/branch_0_fun/all_to_all | solution.py:241
  127.6 18.7 %middle_section.2 = bf16[4096,1024]{1,0:T(8,128)(2,1)} custom-call(bf16[32,128,256]{2,1,0:T(8,128)(2,1)S(1)} %all_to_all.24.refs_0_, bf16[32,128,256]{2,1,0:T(8,128)(2,1)S(1)} %all_to_all.25.refs_1_, bf16[32,128,512]{2,1,0:T(8,128)(2,1)} %all_to_all.26.refs_2_, bf16[256,256]{1,0:T(8,128)(2,1)S(1)} %get-tuple-element.101.refs_3_, ...), custom_call_target="tpu_custom_call" | custom-call | flops 4294967296 | bytes 25165824 | tf_op jit(solution)/shard_map/cond/branch_0_fun/middle_section/pallas_call | solution.py:142
  146.3 76.7 %all_to_all.27.v_ref = bf16[32,128,1024]{2,1,0:T(8,128)(2,1)} all-to-all(bf16[32,128,1024]{2,1,0:T(8,128)(2,1)} %bitcast.12), channel_id=1, replica_groups=mesh['seq'=32,'chan'=4] {'seq'}, dimensions={0} | all-to-all | bytes 16777216 | tf_op jit(solution)/shard_map/cond/branch_0_fun/all_to_all | solution.py:241
  223.0 8.9 %last_section.2 = bf16[4096,1024]{1,0:T(8,128)(2,1)} custom-call(bf16[32,128,1024]{2,1,0:T(8,128)(2,1)} %all_to_all.27.v_ref, bf16[512,512]{1,0:T(8,128)(2,1)S(1)} %get-tuple-element.107.factor_ref), custom_call_target="tpu_custom_call" | custom-call | flops 4294967296 | bytes 16777216 | tf_op jit(solution)/shard_map/cond/branch_0_fun/last_section/pallas_call | solution.py:190
  (18 shorter events, 0.1 us)
Async XLA Ops:
  0.0 9.5 %copy-start.5 = (bf16[256,16]{0,1:T(8,128)(2,1)S(1)}, bf16[256,16]{0,1:T(8,128)(2,1)}, u32[]{:S(2)}) copy-start(bf16[256,16]{0,1:T(8,128)(2,1)} %param.18) | copy-start | bytes 24580
  0.0 9.6 %copy-start.6 = (bf16[8,512]{1,0:T(8,128)(2,1)S(1)}, bf16[8,512]{1,0:T(8,128)(2,1)}, u32[]{:S(2)}) copy-start(bf16[8,512]{1,0:T(8,128)(2,1)} %param.14) | copy-start | bytes 24580
  0.0 10.4 %copy-start.2 = (bf16[512,512]{1,0:T(8,128)(2,1)S(1)}, bf16[512,512]{1,0:T(8,128)(2,1)}, u32[]{:S(2)}) copy-start(bf16[512,512]{1,0:T(8,128)(2,1)} %param.19) | copy-start | bytes 1572868
  0.0 10.4 %copy-start.4 = (bf16[256,256]{1,0:T(8,128)(2,1)S(1)}, bf16[256,256]{1,0:T(8,128)(2,1)}, u32[]{:S(2)}) copy-start(bf16[256,256]{1,0:T(8,128)(2,1)} %param.17) | copy-start | bytes 393220
  0.0 10.4 %copy-start.3 = (bf16[256,256]{1,0:T(8,128)(2,1)S(1)}, bf16[256,256]{1,0:T(8,128)(2,1)}, u32[]{:S(2)}) copy-start(bf16[256,256]{1,0:T(8,128)(2,1)} %param.15) | copy-start | bytes 393220
  0.0 10.4 %copy-start.1 = (bf16[512,512]{1,0:T(8,128)(2,1)S(1)}, bf16[512,512]{1,0:T(8,128)(2,1)}, u32[]{:S(2)}) copy-start(bf16[512,512]{1,0:T(8,128)(2,1)} %param.13) | copy-start | bytes 1572868
  0.0 10.4 %copy-start.7 = (bf16[1024]{0:T(1024)(128)(2,1)S(1)}, bf16[1024]{0:T(1024)(128)(2,1)}, u32[]{:S(2)}) copy-start(bf16[1024]{0:T(1024)(128)(2,1)} %param.12) | copy-start | bytes 6148
  5.3 4.5 %collective-permute-start.2 = (f32[8,512]{1,0:T(8,128)S(1)}, f32[8,512]{1,0:T(8,128)S(1)}, u32[]{:S(2)}, u32[]{:S(2)}) collective-permute-start(f32[8,512]{1,0:T(8,128)S(1)} %reduce_sum.12), channel_id=1, source_target_pairs={{0,3},{1,0},{2,1},{3,2},{4,7},{5,4},{6,5},{7,6},{8,11},{9,8},{10,9... | collective-permute-start | bytes 49160 | tf_op jit(solution)/shard_map/ppermute | solution.py:210
  6.7 3.0 %collective-permute-start.1 = (f32[8,512]{1,0:T(8,128)S(1)}, f32[8,512]{1,0:T(8,128)S(1)}, u32[]{:S(2)}, u32[]{:S(2)}) collective-permute-start(f32[8,512]{1,0:T(8,128)S(1)} %reduce_sum.12), channel_id=1, source_target_pairs={{0,2},{1,3},{2,0},{3,1},{4,6},{5,7},{6,4},{7,5},{8,10},{9,11},{10,... | collective-permute-start | bytes 49160 | tf_op jit(solution)/shard_map/ppermute | solution.py:210
  8.1 2.2 collective-permute-start
  10.4 33.4 %slice-start = ((s8[8388608]{0:T(1024)(128)(4,1)}), s8[4194304]{0:T(1024)(128)(4,1)S(1)}, s32[]{:S(2)}) async-start(s8[8388608]{0:T(1024)(128)(4,1)} %bitcast.10), calls=%async_computation.6 | async-start | bytes 8388608 | tf_op jit(solution)/shard_map/cond
  10.5 33.4 %slice-start.1 = ((s8[8388608]{0:T(1024)(128)(4,1)}), s8[4194304]{0:T(1024)(128)(4,1)S(1)}, s32[]{:S(2)}) async-start(s8[8388608]{0:T(1024)(128)(4,1)} %bitcast.10), calls=%async_computation.7 | async-start | bytes 8388608 | tf_op jit(solution)/shard_map/cond
